TPU v7x, 32 devices: a whole 2x2x4 slice. The times are simulated.
32 devices in a mesh: batch: 8 (over y, x, core), seq: 4 (over z).
Axes of the slice: x: 2, y: 2, z: 4, core: 2. Of those that a mesh axis runs over, the one named last changes fastest.
Arguments:
- hidden_in: bfloat16 [8, 2048, 768], P('batch', 'seq'), may hold values from -6 to 6
- document_ids: int32 [8, 2048], P('batch', 'seq'), may hold values from 0 to 1018, as said below
- query_weight: bfloat16 [768, 768], replicated, may hold values from -0.21875 to 0.21875
- query_bias: float32 [768], replicated, may hold values from -3 to 3
- key_weight: bfloat16 [768, 768], replicated, may hold values from -0.21875 to 0.21875
- value_weight: bfloat16 [768, 768], replicated, may hold values from -0.21875 to 0.21875
- value_bias: float32 [768], replicated, may hold values from -3 to 3
- proj_weight: bfloat16 [768, 768], replicated, may hold values from -0.875 to 0.875
- proj_bias: float32 [768], replicated, may hold values from -3 to 3
- first_gain: float32 [768], replicated, may hold values from 0.5 to 1.5
- first_shift: float32 [768], replicated, may hold values from -3 to 3
- inner_weight: bfloat16 [768, 3072], replicated, may hold values from -0.21875 to 0.21875
- inner_bias: float32 [3072], replicated, may hold values from -3 to 3
- outer_weight: bfloat16 [3072, 768], replicated, may hold values from -0.109375 to 0.109375
- outer_bias: float32 [768], replicated, may hold values from -3 to 3
- second_gain: float32 [768], replicated, may hold values from 0.5 to 1.5
- second_shift: float32 [768], replicated, may hold values from -3 to 3
- output_grad: bfloat16 [8, 2048, 768], P('batch', 'seq'), may hold values from -6 to 6
Outputs:
- output: bfloat16 [8, 2048, 768], P('batch', 'seq')
- grad_hidden: bfloat16 [8, 2048, 768], P('batch', 'seq')
- grad_query_weight: float32 [768, 768], replicated
- grad_query_bias: float32 [768], replicated
- grad_key_weight: float32 [768, 768], replicated
- grad_value_weight: float32 [768, 768], replicated
- grad_value_bias: float32 [768], replicated
- grad_proj_weight: float32 [768, 768], replicated
- grad_proj_bias: float32 [768], replicated
- grad_first_gain: float32 [768], replicated
- grad_first_shift: float32 [768], replicated
- grad_inner_weight: float32 [768, 3072], replicated
- grad_inner_bias: float32 [3072], replicated
- grad_outer_weight: float32 [3072, 768], replicated
- grad_outer_bias: float32 [768], replicated
- grad_second_gain: float32 [768], replicated
- grad_second_shift: float32 [768], replicated
Inputs may be any that keep to these rules, and one draw needn't show every extreme that they name: `document_ids`: along each row of 2048 positions the ids never fall and equal ids stand on consecutive positions. Each row holds one document that begins among its first 512 positions and ends among its last 512; every other document holds at most 512 positions.
All inputs are finite; a program needn't handle non-finite values.
Results may differ from a plain program's by a relative error of at most 0.015.
Values may be sent and summed in bfloat16 or wider, within the bound.
No kernel may reach another device: no remote copies, remote signals or barrier semaphores. Data moves between devices by JAX's collectives and lax.ppermute only.
A program may use at most 192 MiB of HBM per device.

v0:
```python
import jax
import jax.numpy as jnp
from jax import lax
from jax.sharding import PartitionSpec as P

HEADS = 12
HEAD_DIM = 64


EPSILON = 1e-05


def matmul(left, right):
    return jnp.einsum("rtd,de->rte", left, right, preferred_element_type=jnp.float32)


def back_matmul(left, right):
    return jnp.einsum("rte,de->rtd", left, right, preferred_element_type=jnp.float32)


def weight_grad(left, right):
    return jnp.einsum("rtd,rte->de", left, right, preferred_element_type=jnp.float32)


def column_sums(values):
    return jnp.sum(values.astype(jnp.float32), axis=(0, 1))


def layer_norm(values, gain, shift):
    center = values - jnp.mean(values, axis=-1, keepdims=True)
    inverse = lax.rsqrt(jnp.mean(center * center, axis=-1, keepdims=True) + EPSILON)
    scaled = center * inverse
    return (scaled * gain + shift, scaled, inverse)


def norm_back(grad_out, scaled, inverse, gain):
    grad_scaled = grad_out * gain
    grad_in = inverse * (
        grad_scaled
        - jnp.mean(grad_scaled, axis=-1, keepdims=True)
        - scaled * jnp.mean(grad_scaled * scaled, axis=-1, keepdims=True)
    )
    return (grad_in, jnp.sum(grad_out * scaled, axis=(0, 1)), jnp.sum(grad_out, axis=(0, 1)))


def exact_gelu(values):
    return jax.nn.gelu(values, approximate=False)


def split_heads(values):
    return values.reshape(values.shape[0], values.shape[1], HEADS, HEAD_DIM).transpose(2, 0, 1, 3)


def join_heads(values):
    return values.transpose(1, 2, 0, 3).reshape(values.shape[1], values.shape[2], HEADS * HEAD_DIM)


def masked_scores(query_head, key_head, same_doc):
    scores = jnp.einsum("rqe,rke->rqk", query_head, key_head, preferred_element_type=jnp.float32)
    return jnp.where(same_doc, scores * HEAD_DIM ** (-0.5), -1e30)


def shards(
    hidden_in,
    document_ids,
    query_weight,
    query_bias,
    key_weight,
    value_weight,
    value_bias,
    proj_weight,
    proj_bias,
    first_gain,
    first_shift,
    inner_weight,
    inner_bias,
    outer_weight,
    outer_bias,
    second_gain,
    second_shift,
    output_grad,
):
    queries = (matmul(hidden_in, query_weight) + query_bias).astype(jnp.bfloat16)
    key_rows = matmul(hidden_in, key_weight).astype(jnp.bfloat16)
    value_rows = (matmul(hidden_in, value_weight) + value_bias).astype(jnp.bfloat16)
    key_all, value_all, doc_all = (
        lax.all_gather(key_rows, "seq", axis=1, tiled=True),
        lax.all_gather(value_rows, "seq", axis=1, tiled=True),
        lax.all_gather(document_ids, "seq", axis=1, tiled=True),
    )
    same_doc = document_ids[:, :, None] == doc_all[:, None, :]

    def head_forward(operands):
        query_head, key_head, value_head = operands
        scores = masked_scores(query_head, key_head, same_doc)
        row_peak = jnp.max(scores, axis=-1, keepdims=True)
        log_total = row_peak + jnp.log(jnp.sum(jnp.exp(scores - row_peak), axis=-1, keepdims=True))
        attn_prob = jnp.exp(scores - log_total).astype(jnp.bfloat16)
        mixed = jnp.einsum(
            "rqk,rke->rqe", attn_prob, value_head, preferred_element_type=jnp.float32
        )
        return (mixed, log_total)

    attended, log_totals = lax.map(
        head_forward, (split_heads(queries), split_heads(key_all), split_heads(value_all))
    )
    attended = join_heads(attended).astype(jnp.bfloat16)
    branch = matmul(attended, proj_weight) + proj_bias
    first, first_scaled, first_inverse = layer_norm(
        hidden_in.astype(jnp.float32) + branch, first_gain, first_shift
    )
    first_low = first.astype(jnp.bfloat16)
    inner_act = matmul(first_low, inner_weight) + inner_bias
    activated, gelu_back = jax.vjp(exact_gelu, inner_act)
    activated_low = activated.astype(jnp.bfloat16)
    outer_act = matmul(activated_low, outer_weight) + outer_bias
    second, second_scaled, second_inverse = layer_norm(first + outer_act, second_gain, second_shift)
    result = second.astype(jnp.bfloat16)
    grad_mix, grad_second_gain, grad_second_shift = norm_back(
        output_grad.astype(jnp.float32), second_scaled, second_inverse, second_gain
    )
    grad_outer = grad_mix.astype(jnp.bfloat16)
    grad_outer_weight = weight_grad(activated_low, grad_outer)
    grad_outer_bias = column_sums(grad_outer)
    grad_inner = gelu_back(back_matmul(grad_outer, outer_weight))[0].astype(jnp.bfloat16)
    grad_inner_weight = weight_grad(first_low, grad_inner)
    grad_inner_bias = column_sums(grad_inner)
    grad_first = grad_mix + back_matmul(grad_inner, inner_weight)
    grad_resid, grad_first_gain, grad_first_shift = norm_back(
        grad_first, first_scaled, first_inverse, first_gain
    )
    grad_branch = grad_resid.astype(jnp.bfloat16)
    grad_proj_weight = weight_grad(attended, grad_branch)
    grad_proj_bias = column_sums(grad_branch)
    grad_attended = back_matmul(grad_branch, proj_weight).astype(jnp.bfloat16)
    key_all, value_all, doc_all = (
        lax.all_gather(key_rows, "seq", axis=1, tiled=True),
        lax.all_gather(value_rows, "seq", axis=1, tiled=True),
        lax.all_gather(document_ids, "seq", axis=1, tiled=True),
    )
    same_doc = document_ids[:, :, None] == doc_all[:, None, :]

    def head_backward(operands):
        query_head, key_head, value_head, grad_head, log_total = operands
        scores = masked_scores(query_head, key_head, same_doc)
        attn_full = jnp.exp(scores - log_total)
        grad_prob = jnp.einsum(
            "rqe,rke->rqk", grad_head, value_head, preferred_element_type=jnp.float32
        )
        inner_sum = jnp.sum(attn_full * grad_prob, axis=-1, keepdims=True)
        grad_score = (attn_full * (grad_prob - inner_sum)).astype(jnp.bfloat16)
        grad_query = jnp.einsum(
            "rqk,rke->rqe", grad_score, key_head, preferred_element_type=jnp.float32
        )
        grad_key = jnp.einsum(
            "rqk,rqe->rke", grad_score, query_head, preferred_element_type=jnp.float32
        )
        grad_value = jnp.einsum(
            "rqk,rqe->rke",
            attn_full.astype(jnp.bfloat16),
            grad_head,
            preferred_element_type=jnp.float32,
        )
        return (grad_query * HEAD_DIM ** (-0.5), grad_key * HEAD_DIM ** (-0.5), grad_value)

    grad_queries, grad_keys, grad_values = lax.map(
        head_backward,
        (
            split_heads(queries),
            split_heads(key_all),
            split_heads(value_all),
            split_heads(grad_attended),
            log_totals,
        ),
    )
    grad_queries = join_heads(grad_queries).astype(jnp.bfloat16)
    grad_keys, grad_values = (
        lax.psum_scatter(
            join_heads(grad_keys).astype(jnp.bfloat16), "seq", scatter_dimension=1, tiled=True
        ).astype(jnp.float32),
        lax.psum_scatter(
            join_heads(grad_values).astype(jnp.bfloat16), "seq", scatter_dimension=1, tiled=True
        ).astype(jnp.float32),
    )
    grad_keys = grad_keys.astype(jnp.bfloat16)
    grad_values = grad_values.astype(jnp.bfloat16)
    grad_query_weight = weight_grad(hidden_in, grad_queries)
    grad_query_bias = column_sums(grad_queries)
    grad_key_weight = weight_grad(hidden_in, grad_keys)
    grad_value_weight = weight_grad(hidden_in, grad_values)
    grad_value_bias = column_sums(grad_values)
    grad_input = (
        grad_resid
        + back_matmul(grad_queries, query_weight)
        + back_matmul(grad_keys, key_weight)
        + back_matmul(grad_values, value_weight)
    ).astype(jnp.bfloat16)
    (
        grad_query_weight,
        grad_query_bias,
        grad_key_weight,
        grad_value_weight,
        grad_value_bias,
        grad_proj_weight,
        grad_proj_bias,
        grad_first_gain,
        grad_first_shift,
        grad_inner_weight,
        grad_inner_bias,
        grad_outer_weight,
        grad_outer_bias,
        grad_second_gain,
        grad_second_shift,
    ) = lax.psum(
        (
            grad_query_weight,
            grad_query_bias,
            grad_key_weight,
            grad_value_weight,
            grad_value_bias,
            grad_proj_weight,
            grad_proj_bias,
            grad_first_gain,
            grad_first_shift,
            grad_inner_weight,
            grad_inner_bias,
            grad_outer_weight,
            grad_outer_bias,
            grad_second_gain,
            grad_second_shift,
        ),
        ("batch", "seq"),
    )
    return (
        result,
        grad_input,
        grad_query_weight,
        grad_query_bias,
        grad_key_weight,
        grad_value_weight,
        grad_value_bias,
        grad_proj_weight,
        grad_proj_bias,
        grad_first_gain,
        grad_first_shift,
        grad_inner_weight,
        grad_inner_bias,
        grad_outer_weight,
        grad_outer_bias,
        grad_second_gain,
        grad_second_shift,
    )


def solution(mesh):
    placed = (
        P("batch", "seq", None),
        P("batch", "seq"),
        P(),
        P(),
        P(),
        P(),
        P(),
        P(),
        P(),
        P(),
        P(),
        P(),
        P(),
        P(),
        P(),
        P(),
        P(),
        P("batch", "seq", None),
    )
    return jax.shard_map(
        shards,
        mesh=mesh,
        in_specs=placed,
        out_specs=(
            P("batch", "seq", None),
            P("batch", "seq", None),
            P(),
            P(),
            P(),
            P(),
            P(),
            P(),
            P(),
            P(),
            P(),
            P(),
            P(),
            P(),
            P(),
            P(),
            P(),
        ),
        check_vma=False,
    )
```

profile of v0, /device:TPU:0, one launch (start us, length us, event | category | flops | bytes accessed | tf_op | source)
XLA Modules:
  0.0 985.5 jit_solution(14072632175474403634)
XLA Ops:
  7.3 3.3 convolution_convert_fusion.1
  10.7 2.9 add_convert_fusion.2
  17.6 13.9 %all_gather.12 = s32[1,2048]{1,0:T(1,128)S(1)} all-gather(s32[1,512]{1,0:T(1,128)S(1)} %copy-done.17), channel_id=1, replica_groups=mesh['batch'=8,'seq'=4] {'seq'}, dimensions={1}, use_global_device_ids=true | all-gather | bytes 10240 | tf_op jit(solution)/shard_map/all_gather | solution.py:89
  31.5 45.5 %all-gather.5.cloned.1.call-done = bf16[2048,768]{1,0:T(8,128)(2,1)} async-done(((bf16[512,768]{1,0:T(8,128)(2,1)}), bf16[2048,768]{1,0:T(8,128)(2,1)}) %all-gather.5.cloned.1.call-update) | async-done | bytes 3145744 | tf_op jit(solution)/shard_map/all_gather | solution.py:87
  77.0 4.6 copy.43
  81.7 6.7 copy.46
  88.3 53.0 %all-gather.7.cloned.1.call-done = bf16[2048,768]{1,0:T(8,128)(2,1)} async-done(((bf16[512,768]{1,0:T(8,128)(2,1)}), bf16[2048,768]{1,0:T(8,128)(2,1)}) %all-gather.7.cloned.1.call-update) | async-done | bytes 3145744 | tf_op jit(solution)/shard_map/all_gather | solution.py:88
  141.4 4.8 copy.44
  146.1 6.5 copy.47
  152.7 62.5 %while.28 = (s32[]{:T(128)}, bf16[12,1,512,64]{2,3,1,0:T(8,128)(2,1)S(1)}, f32[12,1,512,1]{2,3,1,0:T(1,128)}, bf16[12,1,512,64]{3,2,1,0:T(8,128)(2,1)}, bf16[12,...) while((s32[]{:T(128)}, ...), condition=%wide.region_3.4_spmd.clone, body=%wide.region_0.3_spmd.clone.sunk | while | flops 276823552 | bytes 13924457 | solution.py:104
  216.6 20.4 %multiply_convert_fusion.1 = (bf16[512,3072]{1,0:T(8,128)(2,1)S(1)}, f32[512,3072]{1,0:T(8,128)}, f32[512,3072]{1,0:T(8,128)}) fusion(f32[3072]{0:T(1024)S(1)} %copy-done.31, bf16[768,3072]{1,0:T(8,128)(2,1)} %param.33, f32[1,512,768]{2,1,0:T(8,128)S(1)} %get-tuple-element.286, f32[768]{0:T(1024)S(1)} %copy-done.36, f32[768]{0:T(1024)S(1)} %copy-done.26, ...), kind=kOutput, calls=%fused_computation.56 | convolution fusion | flops 2521694208 | bytes 22042624 | tf_op jit(solution)/shard_map/rtd,de->rte/dot_general | solution.py:14
  237.1 2.8 fusion.90
  243.7 9.9 %convert_reduce_fusion = (f32[3072]{0:T(1024)}, bf16[512,3072]{1,0:T(8,128)(2,1)}) fusion(f32[512,3072]{1,0:T(8,128)} %get-tuple-element.279, bf16[3072,768]{1,0:T(8,128)(2,1)S(1)} %bitcast.228, f32[1,512,768]{2,1,0:T(8,128)S(1)} %get-tuple-element.275, f32[512,3072]{1,0:T(8,128)} %get-tuple-element.287, f32[3072]{0:T(1024)S(1)} %copy-done.31), kind=kOutput, calls=%fused_computation.54 | convolution fusion | flops 2443047936 | bytes 22044672 | tf_op jit(solution)/shard_map/rte,de->rtd/dot_general | solution.py:18
  253.7 5.7 multiply_reduce_fusion.1
  261.7 128.8 %while.29 = (s32[]{:T(128)}, bf16[12,1,512,64]{2,3,1,0:T(8,128)(2,1)S(1)}, bf16[12,1,2048,64]{2,3,1,0:T(8,128)(2,1)}, bf16[12,1,2048,64]{2,3,1,0:T(8,128)(2,1)},...) while((s32[]{:T(128)}, ...), condition=%wide.region_14.15_spmd.clone, body=%wide.region_12.14_spmd.clone.sunk | while | flops 681737728 | bytes 34628736 | solution.py:166
  275.1 2.6 multiply_reduce_fusion.7
  285.8 2.6 multiply_reduce_fusion.7
  296.6 2.6 multiply_reduce_fusion.7
  397.3 5.2 fusion.66
  402.5 5.5 fusion.82
  408.1 41.5 %reduce-scatter.3.cloned.1.call-done = bf16[1,512,768]{1,2,0:T(8,128)(2,1)} async-done(((bf16[1,2048,768]{1,2,0:T(8,128)(2,1)}), bf16[1,512,768]{1,2,0:T(8,128)(2,1)}) %reduce-scatter.3.cloned.1.call-update) | async-done | bytes 786448 | tf_op jit(solution)/shard_map/reduce_scatter | solution.py:178
  449.6 3.3 convolution_bitcast_fusion.2
  452.9 59.2 %reduce-scatter.5.cloned.1.call-done = bf16[1,512,768]{1,2,0:T(8,128)(2,1)} async-done(((bf16[1,2048,768]{1,2,0:T(8,128)(2,1)}), bf16[1,512,768]{1,2,0:T(8,128)(2,1)}) %reduce-scatter.5.cloned.1.call-update) | async-done | bytes 786448 | tf_op jit(solution)/shard_map/reduce_scatter | solution.py:181
  512.1 3.3 convolution_bitcast_fusion.1
  515.8 3.3 fusion.91
  519.3 43.9 %all-reduce = (f32[768]{0:T(1024)}, f32[768]{0:T(1024)}, f32[768]{0:T(1024)}, f32[768]{0:T(1024)}, f32[768]{0:T(1024)}, /*index=5*/f32[3072]{0:T(1024)}, f32[768]{0:T(1024)}, f32[768]{0:T(1024)}, f32[768]{0:T(1024)}) all-reduce(f32[768]{0:T(1024)S(1)} %reduce_sum.182, ...), channel_id=1, replica_groups=mesh['batch'=8,'seq'=4] {'batch','seq'}, use_global_device_ids=true, to_apply=%region_19.20 | all-reduce | flops 9216 | bytes 73728 | tf_op jit(solution)/shard_map/psum | solution.py:214
  565.8 3.1 fusion.55
  568.9 386.8 %all-reduce.4.cloned.1.call-done = (f32[768,768]{0,1:T(8,128)}, f32[768,768]{0,1:T(8,128)}, f32[768,768]{0,1:T(8,128)}, f32[768,768]{1,0:T(8,128)}, f32[768,3072]{1,0:T(8,128)}, /*index=5*/f32[3072,768]{1,0:T(8,128)}) async-done(((f32[768,768]{0,1:T(8,128)}, f32[768,768]{0,1:T(8,128)}, f32[768,768]{0,1:T(8,128)}, f32[768,768]{1,0:T(8,128)}, f32[768,3072]{1,0:T(8,128)}, /*index=5*/f32[3072,768]{1,0:T(8,128)}), ...) | async-done | bytes 28311568 | tf_op jit(solution)/shard_map/psum | solution.py:214
  955.7 3.2 copy.53
  960.8 3.2 copy.55
  965.4 9.3 copy.92
  974.8 3.7 copy.93
  (277 shorter events, 207.5 us)
Async XLA Ops:
  7.2 208.0 %copy-start = (bf16[768,768]{1,0:T(8,128)(2,1)S(1)}, bf16[768,768]{1,0:T(8,128)(2,1)}, u32[]{:S(2)}) copy-start(bf16[768,768]{1,0:T(8,128)(2,1)} %param.29) | copy-start | bytes 3538948
  7.2 69.8 %all-gather.5.cloned.1.call-start = ((), (), s32[]{:S(2)}) async-start(), calls=%async_computation.4 | async-start | bytes 3932160 | tf_op jit(solution)/shard_map/all_gather | solution.py:87
  10.6 130.8 %all-gather.7.cloned.1.call-start = ((), (), s32[]{:S(2)}) async-start(), calls=%async_computation.5 | async-start | bytes 3932160 | tf_op jit(solution)/shard_map/all_gather | solution.py:88
  13.6 436.0 %reduce-scatter.3.cloned.1.call-start = ((), (), s32[]{:S(2)}) async-start(), calls=%async_computation.2 | async-start | bytes 3932160 | tf_op jit(solution)/shard_map/reduce_scatter | solution.py:178
  13.7 3.9 copy-start.17
  152.7 62.5 %copy-start.34 = (f32[768]{0:T(1024)S(1)}, f32[768]{0:T(1024)}, u32[]{:S(2)}) copy-start(f32[768]{0:T(1024)} %param.30) | copy-start | bytes 9220
  215.3 21.8 %slice-start.3 = ((s8[4718592]{0:T(1024)(128)(4,1)}), s8[4194304]{0:T(1024)(128)(4,1)S(1)}, s32[]{:S(2)}) async-start(s8[4718592]{0:T(1024)(128)(4,1)} %bitcast.227), calls=%async_computation.10 | async-start | bytes 8388608
  216.2 43.2 %copy-start.7 = (f32[1,512,768]{2,1,0:T(8,128)}, f32[1,512,768]{2,1,0:T(8,128)S(1)}, u32[]{:S(2)}) copy-start(f32[1,512,768]{2,1,0:T(8,128)S(1)} %get-tuple-element.286) | copy-start | bytes 4718596
  216.6 42.8 %copy-start.24 = (f32[512]{0:T(512)}, f32[512]{0:T(512)S(1)}, u32[]{:S(2)}) copy-start(f32[512]{0:T(512)S(1)} %add_rsqrt_fusion.1) | copy-start | bytes 6148
  216.6 20.5 %slice-start.4 = ((s8[4718592]{0:T(1024)(128)(4,1)}), s8[524288]{0:T(1024)(128)(4,1)S(1)}, s32[]{:S(2)}) async-start(s8[4718592]{0:T(1024)(128)(4,1)} %bitcast.227), calls=%async_computation.11 | async-start | bytes 1048576
  216.6 20.5 %copy-start.35 = (f32[768]{0:T(1024)S(1)}, f32[768]{0:T(1024)}, u32[]{:S(2)}) copy-start(f32[768]{0:T(1024)} %param.36) | copy-start | bytes 9220
  241.6 12.1 %slice-start.5 = ((s8[4718592]{0:T(1024)(128)(4,1)}), s8[4194304]{0:T(1024)(128)(4,1)S(1)}, s32[]{:S(2)}) async-start(s8[4718592]{0:T(1024)(128)(4,1)} %bitcast.229), calls=%async_computation.12 | async-start | bytes 8388608
  243.7 9.9 %copy-start.5 = (f32[1,512,768]{2,1,0:T(8,128)}, f32[1,512,768]{2,1,0:T(8,128)S(1)}, u32[]{:S(2)}) copy-start(f32[1,512,768]{2,1,0:T(8,128)S(1)} %get-tuple-element.275) | copy-start | bytes 4718596
  243.7 10.0 %slice-start.6 = ((s8[4718592]{0:T(1024)(128)(4,1)}), s8[524288]{0:T(1024)(128)(4,1)S(1)}, s32[]{:S(2)}) async-start(s8[4718592]{0:T(1024)(128)(4,1)} %bitcast.229), calls=%async_computation.13 | async-start | bytes 1048576
  390.5 121.5 %reduce-scatter.5.cloned.1.call-start = ((), (), s32[]{:S(2)}) async-start(), calls=%async_computation.3 | async-start | bytes 3932160 | tf_op jit(solution)/shard_map/reduce_scatter | solution.py:181
  391.1 564.6 %all-reduce.4.cloned.1.call-start = ((), (), s32[]{:S(2)}) async-start(), calls=%async_computation.6 | async-start | bytes 56623104 | tf_op jit(solution)/shard_map/psum | solution.py:214
  397.3 5.2 copy-start.8
  397.3 5.2 copy-start.25
  397.3 5.2 copy-start.27
  397.3 5.2 copy-start.37
  397.3 5.3 copy-start.38
  515.4 3.8 copy-start.18
  515.4 3.8 copy-start.19
  515.4 3.8 copy-start.20
  515.5 3.8 copy-start.22
  515.5 3.8 copy-start.23
  515.5 3.8 copy-start.28
  515.5 3.8 copy-start.29
  964.0 10.7 %slice-start = ((s8[9437184]{0:T(1024)(128)(4,1)}), s8[4194304]{0:T(1024)(128)(4,1)S(1)}, s32[]{:S(2)}) async-start(s8[9437184]{0:T(1024)(128)(4,1)} %bitcast.213), calls=%async_computation.7 | async-start | bytes 8388608
  965.4 9.3 slice-start.1
  965.4 9.3 slice-start.2
  974.8 3.8 copy-start.1
  (19 other events, 48.2 us)
Sparse Core Ops, SparseCore 0:
  10.7 66.2 all-gather.4
  79.2 62.1 all-gather.6
  390.7 58.8 reduce-scatter.2
  451.8 60.2 reduce-scatter.4
  519.5 436.1 all-reduce.3
where the time goes:
time: 997 us; the launch traced here: 985 us
  waiting for transfers between devices  587 us (59%)
  matrix products  241 us (24%)
  local copies, waits for them, and re-layouts  64.8 us (6%)
  blocking collectives  57.9 us (6%)
  other arithmetic  19.3 us (2%)
  between operations  14.8 us (1%)
    psum x1, waiting for transfers between devices, shards(): lax.psum((grad_query_weight, grad_query_bias, grad_key_weight, grad_value...  387 us
    reduce_scatter x1, waiting for transfers between devices, shards(): lax.psum_scatter(join_heads(grad_values).astype(jnp.bfloat16), 'seq', sca...  59.2 us
    dot_general x24, matrix products, masked_scores(): jnp.einsum('rqe,rke->rqk', query_head, key_head, preferred_element_type=j...  55.2 us
    all_gather x1, waiting for transfers between devices, shards(): lax.all_gather(value_rows, 'seq', axis=1, tiled=True)  53 us
    all_gather x1, waiting for transfers between devices, shards(): lax.all_gather(key_rows, 'seq', axis=1, tiled=True)  45.5 us
    psum x1, blocking collectives, shards(): lax.psum((grad_query_weight, grad_query_bias, grad_key_weight, grad_value...  43.9 us
    reduce_scatter x1, waiting for transfers between devices, shards(): lax.psum_scatter(join_heads(grad_keys).astype(jnp.bfloat16), 'seq', scatt...  41.5 us
    unnamed x101, local copies, waits for them, and re-layouts  39.4 us
  transfers between devices with their start and end apart: 5, of which 5 were waited for; matrix products, arithmetic and copies ran while one was open for 5% of the time, Pallas kernels for 0%

commit v1 on v0

v1 whole, which is shorter than its diff:
```python
import functools
import jax
import jax.numpy as jnp
from jax import lax
from jax.experimental import pallas as pl
from jax.experimental.pallas import tpu as pltpu
from jax.sharding import PartitionSpec as P

HEAD_DIM = 64
PAIR = 128
MASKED = -1e30

NT = (((1,), (1,)), ((), ()))
NN = (((1,), (0,)), ((), ()))


def dot(left, right, dims):
    return lax.dot_general(left, right, dims, preferred_element_type=jnp.float32)


def lane_half(x, half):
    lanes = lax.broadcasted_iota(jnp.int32, x.shape, 1)
    keep = lanes < HEAD_DIM if half == 0 else lanes >= HEAD_DIM
    return jnp.where(keep, x, jnp.zeros_like(x))


def fill_bias(bias_ref, kind_ref, ids_q_ref, ids_k_ref, slots, block):
    for slot in range(slots):

        @pl.when(kind_ref[slot] == 2)
        def _():
            same = ids_k_ref[pl.ds(slot * block, block), :] == ids_q_ref[...]
            bias_ref[slot] = jnp.where(same, 0.0, MASKED)


def forward_kernel(
    slots, block, first, kind_ref, q_ref, k_ref, v_ref, ids_q_ref, ids_k_ref, *refs
):
    if first:
        acc_out, peak_out, sum_out, bias_ref = refs
        acc_out[...] = jnp.zeros_like(acc_out)
        sum_out[...] = jnp.zeros_like(sum_out)
        peak_out[...] = jnp.full(peak_out.shape, MASKED, jnp.float32)
    else:
        acc_in, peak_in, sum_in, acc_out, peak_out, sum_out, bias_ref = refs
        acc_out[...] = acc_in[...]
        sum_out[...] = sum_in[...]
        peak_out[...] = peak_in[...]

    @pl.when(pl.program_id(0) == 0)
    def _():
        fill_bias(bias_ref, kind_ref, ids_q_ref, ids_k_ref, slots, block)

    q = q_ref[...]
    ones = jnp.ones((16, block), jnp.bfloat16)
    for slot in range(slots):

        def visit(masked):
            k = k_ref[pl.ds(slot * block, block), :]
            v_t = v_ref[pl.ds(slot * block, block), :].T
            scores = [dot(k, lane_half(q, half), NT) for half in range(2)]
            if masked:
                scores = [x + bias_ref[slot] for x in scores]
            old = [peak_out[0, half : half + 1, :] for half in range(2)]
            peak = [jnp.maximum(o, jnp.max(x, axis=0, keepdims=True)) for o, x in zip(old, scores)]
            prob = [jnp.exp(x - m).astype(jnp.bfloat16) for x, m in zip(scores, peak)]
            for half in range(2):
                shrink = jnp.exp(old[half] - peak[half])
                rows = slice(half * HEAD_DIM, (half + 1) * HEAD_DIM)
                mixed = dot(jnp.concatenate([v_t[rows], ones], axis=0), prob[half], NN)
                acc_out[rows, :] = acc_out[rows, :] * shrink + mixed[:HEAD_DIM]
                sum_out[0, half : half + 1, :] = (
                    sum_out[0, half : half + 1, :] * shrink + mixed[HEAD_DIM : HEAD_DIM + 1]
                )
                peak_out[0, half : half + 1, :] = peak[half]

        pl.when(kind_ref[slot] == 1)(functools.partial(visit, False))
        pl.when(kind_ref[slot] == 2)(functools.partial(visit, True))


def attend_forward(kinds, q, k, v, ids_q, ids_k, state):
    block, width = q.shape
    slots = k.shape[0] // block
    pairs = width // PAIR
    rows = pl.BlockSpec((1, 2, block), lambda p, kinds: (p, 0, 0))
    acc = pl.BlockSpec((PAIR, block), lambda p, kinds: (p, 0))
    state_specs = [acc, rows, rows]
    in_specs = [
        pl.BlockSpec((block, PAIR), lambda p, kinds: (0, p)),
        pl.BlockSpec((slots * block, PAIR), lambda p, kinds: (0, p)),
        pl.BlockSpec((slots * block, PAIR), lambda p, kinds: (0, p)),
        pl.BlockSpec((1, block), lambda p, kinds: (0, 0)),
        pl.BlockSpec((slots * block, 1), lambda p, kinds: (0, 0)),
    ]
    out_shape = [
        jax.ShapeDtypeStruct((width, block), jnp.float32),
        jax.ShapeDtypeStruct((pairs, 2, block), jnp.float32),
        jax.ShapeDtypeStruct((pairs, 2, block), jnp.float32),
    ]
    first = state is None
    return pl.pallas_call(
        functools.partial(forward_kernel, slots, block, first),
        grid_spec=pltpu.PrefetchScalarGridSpec(
            num_scalar_prefetch=1,
            grid=(pairs,),
            in_specs=in_specs + ([] if first else state_specs),
            out_specs=state_specs,
            scratch_shapes=[pltpu.VMEM((slots, block, block), jnp.float32)],
        ),
        out_shape=out_shape,
        compiler_params=pltpu.CompilerParams(vmem_limit_bytes=48 * 2**20),
        cost_estimate=pl.CostEstimate(
            flops=int(4 * slots * block * block * width * 2),
            bytes_accessed=int(4 * slots * block * width + 8 * block * width),
            transcendentals=0,
        ),
        name="attend_forward",
    )(kinds, q, k, v, ids_q, ids_k, *([] if first else state))


def backward_kernel(
    slots, block, first, kind_ref, q_ref, g_ref, k_ref, v_ref, total_ref, delta_ref, ids_q_ref, ids_k_ref, *refs
):
    if first:
        grad_q, grad_k, grad_v, bias_ref = refs
        grad_q[...] = jnp.zeros_like(grad_q)
    else:
        grad_q_in, grad_q, grad_k, grad_v, bias_ref = refs
        grad_q[...] = grad_q_in[...]

    @pl.when(pl.program_id(0) == 0)
    def _():
        fill_bias(bias_ref, kind_ref, ids_q_ref, ids_k_ref, slots, block)

    q, g = q_ref[...], g_ref[...]
    for slot in range(slots):
        here = pl.ds(slot * block, block)

        def visit(masked):
            k, v = k_ref[here, :], v_ref[here, :]
            k_t = k.T
            sum_k = sum_v = None
            for half in range(2):
                q_half, g_half = lane_half(q, half), lane_half(g, half)
                scores = dot(k, q_half, NT)
                if masked:
                    scores = scores + bias_ref[slot]
                prob = jnp.exp(scores - total_ref[0, half : half + 1, :])
                grad_prob = dot(v, g_half, NT)
                grad_score = (prob * (grad_prob - delta_ref[0, half : half + 1, :])).astype(jnp.bfloat16)
                part_v = dot(prob.astype(jnp.bfloat16), g_half, NN)
                part_k = dot(grad_score, q_half, NN)
                sum_v = part_v if sum_v is None else sum_v + part_v
                sum_k = part_k if sum_k is None else sum_k + part_k
                rows = slice(half * HEAD_DIM, (half + 1) * HEAD_DIM)
                grad_q[rows, :] += dot(k_t[rows], grad_score, NN)
            grad_k[here, :] = sum_k.astype(jnp.bfloat16)
            grad_v[here, :] = sum_v.astype(jnp.bfloat16)

        pl.when(kind_ref[slot] == 1)(functools.partial(visit, False))
        pl.when(kind_ref[slot] == 2)(functools.partial(visit, True))

        @pl.when(kind_ref[slot] == 0)
        def _():
            grad_k[here, :] = jnp.zeros((block, PAIR), jnp.bfloat16)
            grad_v[here, :] = jnp.zeros((block, PAIR), jnp.bfloat16)


def attend_backward(kinds, q, g, k, v, totals, deltas, ids_q, ids_k, grad_q):
    block, width = q.shape
    slots = k.shape[0] // block
    pairs = width // PAIR
    rows = pl.BlockSpec((1, 2, block), lambda p, kinds: (p, 0, 0))
    acc = pl.BlockSpec((PAIR, block), lambda p, kinds: (p, 0))
    mine = pl.BlockSpec((block, PAIR), lambda p, kinds: (0, p))
    theirs = pl.BlockSpec((slots * block, PAIR), lambda p, kinds: (0, p))
    first = grad_q is None
    return pl.pallas_call(
        functools.partial(backward_kernel, slots, block, first),
        grid_spec=pltpu.PrefetchScalarGridSpec(
            num_scalar_prefetch=1,
            grid=(pairs,),
            in_specs=[mine, mine, theirs, theirs, rows, rows]
            + [
                pl.BlockSpec((1, block), lambda p, kinds: (0, 0)),
                pl.BlockSpec((slots * block, 1), lambda p, kinds: (0, 0)),
            ]
            + ([] if first else [acc]),
            out_specs=[acc, theirs, theirs],
            scratch_shapes=[pltpu.VMEM((slots, block, block), jnp.float32)],
        ),
        out_shape=[
            jax.ShapeDtypeStruct((width, block), jnp.float32),
            jax.ShapeDtypeStruct((slots * block, width), jnp.bfloat16),
            jax.ShapeDtypeStruct((slots * block, width), jnp.bfloat16),
        ],
        compiler_params=pltpu.CompilerParams(vmem_limit_bytes=48 * 2**20),
        cost_estimate=pl.CostEstimate(
            flops=int(10 * slots * block * block * width * 2),
            bytes_accessed=int(8 * slots * block * width + 12 * block * width),
            transcendentals=0,
        ),
        name="attend_backward",
    )(kinds, q, g, k, v, totals, deltas, ids_q, ids_k, *([] if first else [grad_q]))


EPSILON = 1e-05
ROOT_HALF = 0.7071067811865476
ROOT_TAU = 0.3989422804014327


def low(x):
    return x.astype(jnp.bfloat16)


def times(left, right):
    return dot(left, right, NN)


def times_back(left, right):
    return dot(left, right, NT)


def weight_grad(left, right):
    return dot(left, right, (((0,), (0,)), ((), ())))


def column_sums(x):
    return jnp.sum(x.astype(jnp.float32), axis=0)


def layer_norm(values, gain, shift):
    center = values - jnp.mean(values, axis=-1, keepdims=True)
    inverse = lax.rsqrt(jnp.mean(center * center, axis=-1, keepdims=True) + EPSILON)
    scaled = center * inverse
    return scaled * gain + shift, scaled, inverse


def norm_back(grad_out, scaled, inverse, gain):
    grad_scaled = grad_out * gain
    grad_in = inverse * (
        grad_scaled
        - jnp.mean(grad_scaled, axis=-1, keepdims=True)
        - scaled * jnp.mean(grad_scaled * scaled, axis=-1, keepdims=True)
    )
    return grad_in, jnp.sum(grad_out * scaled, axis=0), jnp.sum(grad_out, axis=0)


def swap(x, bit, count):
    return lax.ppermute(x, "batch", [(i, i ^ bit) for i in range(count)])


def pick(x, index, parts, axis):
    size = x.shape[axis] // parts
    return lax.dynamic_slice_in_dim(x, index * size, size, axis)


def add_low(left, right):
    return low(left.astype(jnp.float32) + right.astype(jnp.float32))


def halve(x, bit, count):
    side = (lax.axis_index("batch") // bit) % 2
    return add_low(pick(x, side, 2, 0), swap(pick(x, 1 - side, 2, 0), bit, count))


def unhalve(x, bit, count):
    side = (lax.axis_index("batch") // bit) % 2
    other = swap(x, bit, count)
    return jnp.where(
        side == 0, jnp.concatenate([x, other], axis=0), jnp.concatenate([other, x], axis=0)
    )


def turn(x, distance, count):
    return lax.ppermute(x, "seq", [(i, (i + distance) % count) for i in range(count)])


def reduce_all(x, batch, seq):
    bits = [1 << i for i in range(batch.bit_length() - 1)]
    rest = bits[1:]
    orders = (rest, rest[::-1])
    half = halve(x, 1, batch)
    sides = list(jnp.split(half, 2, axis=0))
    for step in range(len(rest)):
        sides = [halve(side, order[step], batch) for side, order in zip(sides, orders)]
    held = jnp.concatenate(sides, axis=1)
    me = lax.axis_index("seq")
    total = pick(held, me, seq, 1).astype(jnp.float32)
    for distance in range(1, seq):
        total += turn(pick(held, (me + distance) % seq, seq, 1), distance, seq).astype(jnp.float32)
    mine = low(total)
    around = [mine] + [turn(mine, seq - step, seq) for step in range(1, seq)]
    width = mine.shape[1]
    ahead = jnp.concatenate(around + around, axis=1)
    held = lax.dynamic_slice_in_dim(ahead, ((seq - me) % seq) * width, seq * width, 1)
    sides = list(jnp.split(held, 2, axis=1))
    for step in reversed(range(len(rest))):
        sides = [unhalve(side, order[step], batch) for side, order in zip(sides, orders)]
    return unhalve(jnp.concatenate(sides, axis=0), 1, batch).astype(jnp.float32)


def reduce_small(x, batch, seq):
    for i in range(batch.bit_length() - 1):
        x = x + swap(x, 1 << i, batch)
    return x + sum(turn(x, distance, seq) for distance in range(1, seq))


def kind_of(valid, ids_q, ids_k):
    apart = (ids_q[-1] < ids_k[0]) | (ids_k[-1] < ids_q[0])
    one = (ids_q[0] == ids_k[-1]) & (ids_q[-1] == ids_k[0])
    return jnp.where(jnp.logical_not(valid) | apart, 0, jnp.where(one, 1, 2)).astype(jnp.int32)


def shards(
    batch,
    seq,
    hidden_in,
    document_ids,
    query_weight,
    query_bias,
    key_weight,
    value_weight,
    value_bias,
    proj_weight,
    proj_bias,
    first_gain,
    first_shift,
    inner_weight,
    inner_bias,
    outer_weight,
    outer_bias,
    second_gain,
    second_shift,
    output_grad,
):
    hidden = hidden_in[0]
    ids = document_ids[0]
    grad_out = output_grad[0].astype(jnp.float32)
    block, width = hidden.shape
    heads = width // HEAD_DIM
    me = lax.axis_index("seq")
    scale = HEAD_DIM ** (-0.5)

    steps = []
    left, right = (hidden, ids), (hidden, ids)
    for s in range(1, seq):
        to_right = [(i, i + 1) for i in range(s - 1, seq - 1)]
        to_left = [(i, i - 1) for i in range(1, seq - s + 1)]
        left = tuple(lax.ppermute(x, "seq", to_right) for x in left)
        right = tuple(lax.ppermute(x, "seq", to_left) for x in right)
        has_left, has_right = me >= s, me + s <= seq - 1
        if 2 * s <= seq - 1:
            slots = [(has_left,) + left, (has_right,) + right]
        else:
            slots = [
                (has_left | has_right,)
                + tuple(jnp.where(has_left, a, b) for a, b in zip(left, right))
            ]
        steps.append(slots)
    groups = [[(me >= 0, hidden, ids)]] + steps

    queries = low((times(hidden, query_weight) + query_bias)) * jnp.bfloat16(scale)
    ids_q = ids[None, :]
    state = None
    kept = []
    for slots in groups:
        tokens = jnp.concatenate([slot[1] for slot in slots], axis=0)
        ids_k = jnp.concatenate([slot[2] for slot in slots], axis=0)
        kinds = jnp.stack([kind_of(slot[0], ids, slot[2]) for slot in slots])
        keys = low(times(tokens, key_weight))
        values = low(times(tokens, value_weight) + value_bias)
        state = attend_forward(kinds, queries, keys, values, ids_q, ids_k[:, None], state)
        kept.append((kinds, tokens, keys, values, ids_k[:, None]))
    acc, peak, sums = state
    attended_t = acc.reshape(heads, HEAD_DIM, block) / sums.reshape(heads, 1, block)
    attended_full = attended_t.reshape(width, block).T
    attended = low(attended_full)
    totals = peak + jnp.log(sums)

    branch = times(attended, proj_weight) + proj_bias
    first, first_scaled, first_inverse = layer_norm(
        hidden.astype(jnp.float32) + branch, first_gain, first_shift
    )
    first_low = low(first)
    inner_act = times(first_low, inner_weight) + inner_bias
    chance = 0.5 * (1.0 + lax.erf(inner_act * ROOT_HALF))
    activated = low(inner_act * chance)
    slope = chance + inner_act * (ROOT_TAU * jnp.exp(-0.5 * inner_act * inner_act))
    outer_act = times(activated, outer_weight) + outer_bias
    second, second_scaled, second_inverse = layer_norm(first + outer_act, second_gain, second_shift)
    result = low(second)
    grad_mix, grad_second_gain, grad_second_shift = norm_back(
        grad_out, second_scaled, second_inverse, second_gain
    )
    grad_outer = low(grad_mix)
    grad_outer_weight = reduce_all(low(weight_grad(activated, grad_outer)), batch, seq)
    grad_outer_bias = column_sums(grad_outer)
    grad_inner = low(times_back(grad_outer, outer_weight) * slope)
    grad_inner_bias = column_sums(grad_inner)
    grad_first = grad_mix + times_back(grad_inner, inner_weight)
    grad_resid, grad_first_gain, grad_first_shift = norm_back(
        grad_first, first_scaled, first_inverse, first_gain
    )
    grad_branch = low(grad_resid)
    grad_proj_bias = column_sums(grad_branch)
    early = reduce_all(
        jnp.concatenate(
            [low(weight_grad(first_low, grad_inner)), low(weight_grad(attended, grad_branch))], axis=1
        ),
        batch,
        seq,
    )
    grad_inner_weight, grad_proj_weight = jnp.split(early, [inner_weight.shape[1]], axis=1)
    grad_attended = low(times_back(grad_branch, proj_weight))
    deltas = jnp.sum(
        (grad_attended.astype(jnp.float32) * attended_full).reshape(block, heads, HEAD_DIM), axis=-1
    ).T.reshape(heads // 2, 2, block)

    grad_query_t = None
    grad_key_weight = grad_value_weight = grad_value_bias = 0.0
    to_left = to_right = None
    for s in reversed(range(seq)):
        kinds, tokens, keys, values, ids_k = kept[s]
        grad_query_t, grad_keys, grad_values = attend_backward(
            kinds, queries, grad_attended, keys, values, totals, deltas, ids_q, ids_k, grad_query_t
        )
        grad_key_weight += weight_grad(tokens, grad_keys)
        grad_value_weight += weight_grad(tokens, grad_values)
        grad_value_bias += column_sums(grad_values)
        terms = times_back(grad_keys, key_weight) + times_back(grad_values, value_weight)
        if s == 0:
            own_terms = terms
            break
        has_left, has_right = me >= s, me + s <= seq - 1
        if len(steps[s - 1]) == 2:
            left_terms, right_terms = jnp.split(terms, 2, axis=0)
        else:
            left_terms = jnp.where(has_left, terms, 0.0)
            right_terms = jnp.where(has_right, terms, 0.0)
        if to_left is not None:
            left_terms = left_terms + to_left.astype(jnp.float32)
            right_terms = right_terms + to_right.astype(jnp.float32)
        to_left = lax.ppermute(low(left_terms), "seq", [(i, i - 1) for i in range(s, seq)])
        to_right = lax.ppermute(low(right_terms), "seq", [(i, i + 1) for i in range(seq - s)])
    grad_queries = low(grad_query_t * scale).T
    grad_query_weight = weight_grad(hidden, grad_queries)
    grad_query_bias = column_sums(grad_queries)
    own_terms = own_terms + grad_resid + times_back(grad_queries, query_weight)
    if to_left is not None:
        own_terms = own_terms + to_left.astype(jnp.float32) + to_right.astype(jnp.float32)
    grad_input = low(own_terms)
    late = reduce_all(
        jnp.concatenate([low(grad_query_weight), low(grad_key_weight), low(grad_value_weight)], axis=1),
        batch,
        seq,
    )
    grad_query_weight, grad_key_weight, grad_value_weight = jnp.split(late, 3, axis=1)

    small = [
        grad_query_bias,
        grad_value_bias,
        grad_proj_bias,
        grad_first_gain,
        grad_first_shift,
        grad_outer_bias,
        grad_second_gain,
        grad_second_shift,
        grad_inner_bias,
    ]
    together = reduce_small(jnp.concatenate(small), batch, seq)
    sizes = [x.shape[0] for x in small]
    cuts = [sum(sizes[: i + 1]) for i in range(len(sizes) - 1)]
    (
        grad_query_bias,
        grad_value_bias,
        grad_proj_bias,
        grad_first_gain,
        grad_first_shift,
        grad_outer_bias,
        grad_second_gain,
        grad_second_shift,
        grad_inner_bias,
    ) = jnp.split(together, cuts)
    return (
        result[None],
        grad_input[None],
        grad_query_weight,
        grad_query_bias,
        grad_key_weight,
        grad_value_weight,
        grad_value_bias,
        grad_proj_weight,
        grad_proj_bias,
        grad_first_gain,
        grad_first_shift,
        grad_inner_weight,
        grad_inner_bias,
        grad_outer_weight,
        grad_outer_bias,
        grad_second_gain,
        grad_second_shift,
    )


def solution(mesh):
    rows = P("batch", "seq", None)
    return jax.shard_map(
        functools.partial(shards, mesh.shape["batch"], mesh.shape["seq"]),
        mesh=mesh,
        in_specs=(rows, P("batch", "seq")) + (P(),) * 15 + (rows,),
        out_specs=(rows, rows) + (P(),) * 15,
        check_vma=False,
    )
```

time: 997 us -> 538 us (0.54)
  waiting for transfers between devices: 587 us -> 168 us
  matrix products: 241 us -> 74.4 us
  starting transfers between devices: 0.2 us -> 100 us
  Pallas kernels: 0 us -> 77.4 us
  blocking collectives: 57.9 us -> 0 us
  local copies, waits for them, and re-layouts: 64.8 us -> 48.1 us
  other arithmetic: 19.3 us -> 32.7 us
  between operations: 14.8 us -> 28 us
    psum x1 -> x0, waiting for transfers between devices: 387 us -> none  [shards(): lax.psum((grad_query_weight, grad_query_bias, grad_key_weight, grad_value...]
    ppermute x0 -> x72, waiting for transfers between devices: none -> 168 us  [the longest x33 65.3 us: swap(): return lax.ppermute(x, 'batch', [(i, i ^ bit) for i in range(count)])]
    dot_general x102 -> x36, matrix products: 241 us -> 74.4 us  [dot(): lax.dot_general(left, right, dims, preferred_element_type=jnp.float32)]
    reduce_scatter x2 -> x0, waiting for transfers between devices: 101 us -> none  [the longest x1 59.2 us: shards(): lax.psum_scatter(join_heads(grad_values).astype(jnp.bfloat16), 'seq', sca...]
    ppermute x0 -> x72, starting transfers between devices: none -> 100 us  [the longest x33 34.4 us: swap(): return lax.ppermute(x, 'batch', [(i, i ^ bit) for i in range(count)])]
    all_gather x2 -> x0, waiting for transfers between devices: 98.6 us -> none  [the longest x1 53 us: shards(): lax.all_gather(value_rows, 'seq', axis=1, tiled=True)]
    pallas_call x0 -> x8, Pallas kernels: none -> 77.4 us  [the longest x4 49.9 us: attend_backward(): pl.pallas_call(functools.partial(backward_kernel, slots, block, first), g...]
    psum x1 -> x0, blocking collectives: 43.9 us -> none  [shards(): lax.psum((grad_query_weight, grad_query_bias, grad_key_weight, grad_value...]
  transfers between devices with their start and end apart: 5 -> 72, of which waited for: 5 -> 34; matrix products, arithmetic and copies ran while one was open for 5% -> 12% of each run, Pallas kernels for 0% -> 4%
where the time goes in v1:
time: 538 us; the launch traced here: 529 us
  waiting for transfers between devices  168 us (31%)
  starting transfers between devices  100 us (19%)
  Pallas kernels  77.4 us (14%)
  matrix products  74.4 us (14%)
  local copies, waits for them, and re-layouts  48.1 us (9%)
  other arithmetic  32.7 us (6%)
  between operations  28 us (5%)
    dot_general x36, matrix products, dot(): lax.dot_general(left, right, dims, preferred_element_type=jnp.float32)  74.4 us
    ppermute x33, waiting for transfers between devices, swap(): return lax.ppermute(x, 'batch', [(i, i ^ bit) for i in range(count)])  65.3 us
    pallas_call x4, Pallas kernels, attend_backward(): pl.pallas_call(functools.partial(backward_kernel, slots, block, first), g...  49.9 us
    ppermute x21, waiting for transfers between devices, turn(): lax.ppermute(x, 'seq', [(i, (i + distance) % count) for i in range(count)])  47.6 us
    ppermute x33, starting transfers between devices, swap(): return lax.ppermute(x, 'batch', [(i, i ^ bit) for i in range(count)])  34.4 us
    ppermute x21, starting transfers between devices, turn(): lax.ppermute(x, 'seq', [(i, (i + distance) % count) for i in range(count)])  33.1 us
    pallas_call x4, Pallas kernels, attend_forward(): pl.pallas_call(functools.partial(forward_kernel, slots, block, first), gr...  27.5 us
    ppermute x6, waiting for transfers between devices, shards(): right = tuple((lax.ppermute(x, 'seq', to_left) for x in right))  23 us
  transfers between devices with their start and end apart: 72, of which 34 were waited for; matrix products, arithmetic and copies ran while one was open for 12% of the time, Pallas kernels for 4%

profile of v1, /device:TPU:0, one launch (start us, length us, event | category | flops | bytes accessed | tf_op | source)
XLA Modules:
  0.0 528.5 jit_solution(8534254804470017144)
XLA Ops:
  0.7 5.1 collective-permute-start
  7.0 5.5 %collective-permute-start.6 = (bf16[512,768]{1,0:T(8,128)(2,1)}, bf16[512,768]{1,0:T(8,128)(2,1)}, u32[]{:S(2)}, u32[]{:S(2)}) collective-permute-start(bf16[512,768]{1,0:T(8,128)(2,1)} %bitcast.138), channel_id=1, source_target_pairs={{0,1},{1,2},{2,3},{4,5},{5,6},{6,7},{8,9},{9,10},{10,11},{12,13},{... | collective-permute-start | bytes 2359304 | tf_op jit(solution)/shard_map/ppermute | solution.py:350
  27.1 6.4 %attend_forward.4 = (f32[768,512]{1,0:T(8,128)S(1)}, f32[6,2,512]{2,1,0:T(2,128)S(1)}, f32[6,2,512]{2,1,0:T(2,128)S(1)}) custom-call(s32[1]{0:T(128)} %bitcast.19.kind_ref, bf16[512,768]{1,0:T(8,128)(2,1)S(1)} %fusion.26.q_ref, bf16[512,768]{1,0:T(8,128)(2,1)S(1)} %convolution_convert_fusion.6.k_ref, bf16[512,768]{1,0:T(8,128)(2,1)S(1)} %add_convert_fusion.8.v_ref, ...), custom_call_target="tpu_custom_call" | custom-call | flops 1610612736 | bytes 4718592 | tf_op jit(solution)/shard_map/attend_forward/pallas_call | solution.py:101
  50.2 5.6 %collective-permute-done.4 = s32[512]{0:T(512)S(1)} collective-permute-done((s32[512]{0:T(512)S(1)}, s32[512]{0:T(512)S(1)}, u32[]{:S(2)}, u32[]{:S(2)}) %collective-permute-start.4) | collective-permute-done | bytes 2080 | tf_op jit(solution)/shard_map/ppermute | solution.py:351
  77.1 8.2 %attend_forward.5 = (f32[768,512]{1,0:T(8,128)S(1)}, f32[6,2,512]{2,1,0:T(2,128)S(1)}, f32[6,2,512]{2,1,0:T(2,128)S(1)}) custom-call(s32[2]{0:T(128)S(1)} %pad_add_fusion.1.kind_ref, bf16[512,768]{1,0:T(8,128)(2,1)S(1)} %fusion.26.q_ref, bf16[1024,768]{1,0:T(8,128)(2,1)S(1)} %convolution_convert_fusion.2.k_ref, ...), custom_call_target="tpu_custom_call" | custom-call | flops 3221225472 | bytes 6291456 | tf_op jit(solution)/shard_map/attend_forward/pallas_call | solution.py:101
  86.0 7.7 %collective-permute-done.10 = bf16[512,768]{1,0:T(8,128)(2,1)S(1)} collective-permute-done((bf16[512,768]{1,0:T(8,128)(2,1)}, bf16[512,768]{1,0:T(8,128)(2,1)S(1)}, u32[]{:S(2)}, u32[]{:S(2)}) %collective-permute-start.10) | collective-permute-done | bytes 786464 | tf_op jit(solution)/shard_map/ppermute | solution.py:351
  97.4 6.4 %attend_forward.6 = (f32[768,512]{1,0:T(8,128)S(1)}, f32[6,2,512]{2,1,0:T(2,128)S(1)}, f32[6,2,512]{2,1,0:T(2,128)S(1)}) custom-call(s32[1]{0:T(128)} %bitcast.10.kind_ref, bf16[512,768]{1,0:T(8,128)(2,1)S(1)} %fusion.26.q_ref, bf16[512,768]{1,0:T(8,128)(2,1)S(1)} %convolution_convert_fusion.7.k_ref, bf16[512,768]{1,0:T(8,128)(2,1)S(1)} %add_convert_fusion.9.v_ref, ...), custom_call_target="tpu_custom_call" | custom-call | flops 1610612736 | bytes 4718592 | tf_op jit(solution)/shard_map/attend_forward/pallas_call | solution.py:101
  103.8 9.6 %collective-permute-done.11 = bf16[512,768]{1,0:T(8,128)(2,1)S(1)} collective-permute-done((bf16[512,768]{1,0:T(8,128)(2,1)S(1)}, bf16[512,768]{1,0:T(8,128)(2,1)S(1)}, u32[]{:S(2)}, u32[]{:S(2)}) %collective-permute-start.11) | collective-permute-done | bytes 786464 | tf_op jit(solution)/shard_map/ppermute | solution.py:351
  115.9 6.4 %attend_forward.7 = (f32[768,512]{1,0:T(8,128)S(1)}, f32[6,2,512]{2,1,0:T(2,128)S(1)}, f32[6,2,512]{2,1,0:T(2,128)S(1)}) custom-call(s32[1]{0:T(128)} %bitcast.6.kind_ref, bf16[512,768]{1,0:T(8,128)(2,1)S(1)} %copy-done.17, bf16[512,768]{1,0:T(8,128)(2,1)S(1)} %convolution_convert_fusion.8.k_ref, bf16[512,768]{1,0:T(8,128)(2,1)S(1)} %add_convert_fusion.10.v_ref, ...), custom_call_target="tpu_custom_call" | custom-call | flops 1610612736 | bytes 4718592 | tf_op jit(solution)/shard_map/attend_forward/pallas_call | solution.py:101
  134.3 6.5 %multiply_convert_fusion = (bf16[512,3072]{1,0:T(8,128)(2,1)S(1)}, f32[512,3072]{1,0:T(8,128)S(1)}) fusion(f32[3072]{0:T(1024)S(1)} %copy-done.74, bf16[768,3072]{1,0:T(8,128)(2,1)} %param.29, f32[512,768]{1,0:T(8,128)S(1)} %get-tuple-element.166, f32[768]{0:T(1024)S(1)} %copy-done.79, f32[768]{0:T(1024)S(1)} %copy-done.64, f32[512]{0:T(512)S(1)} %add_rsqrt_fusion.1, ...), kind=kOutput, calls=%fused_computation.10 | convolution fusion | flops 2427322368 | bytes 15751168 | tf_op jit(solution)/shard_map/dot_general | solution.py:18
  148.2 5.3 %convert_reduce_fusion = (f32[3072]{0:T(1024)}, bf16[512,3072]{1,0:T(8,128)(2,1)S(1)}) fusion(f32[512,3072]{1,0:T(8,128)S(1)} %get-tuple-element.168, f32[3072]{0:T(1024)S(1)} %copy-done.74, bf16[3072,768]{1,0:T(8,128)(2,1)S(1)} %bitcast.147, f32[512,768]{1,0:T(8,128)S(1)} %get-tuple-element.111), kind=kOutput, calls=%fused_computation.9 | convolution fusion | flops 2436756480 | bytes 15753216 | tf_op jit(solution)/shard_map/dot_general | solution.py:18
  170.0 11.4 %attend_backward.4 = (f32[768,512]{1,0:T(8,128)}, bf16[512,768]{1,0:T(8,128)(2,1)S(1)}, bf16[512,768]{1,0:T(8,128)(2,1)S(1)}) custom-call(s32[1]{0:T(128)} %bitcast.6.kind_ref, bf16[512,768]{1,0:T(8,128)(2,1)S(1)} %copy-done.18, bf16[512,768]{1,0:T(8,128)(2,1)S(1)} %get-tuple-element.173.g_ref, bf16[512,768]{1,0:T(8,128)(2,1)S(1)} %copy-done.15, ...), custom_call_target="tpu_custom_call" | custom-call | flops 4026531840 | bytes 7864320 | tf_op jit(solution)/shard_map/attend_backward/pallas_call | solution.py:178
  181.5 12.3 %attend_backward.5 = (f32[768,512]{1,0:T(8,128)}, bf16[512,768]{1,0:T(8,128)(2,1)S(1)}, bf16[512,768]{1,0:T(8,128)(2,1)S(1)}) custom-call(s32[1]{0:T(128)} %bitcast.10.kind_ref, bf16[512,768]{1,0:T(8,128)(2,1)S(1)} %copy-done.19, bf16[512,768]{1,0:T(8,128)(2,1)S(1)} %get-tuple-element.173.g_ref, bf16[512,768]{1,0:T(8,128)(2,1)S(1)} %copy-done.13, ...), custom_call_target="tpu_custom_call" | custom-call | flops 4026531840 | bytes 7864320 | tf_op jit(solution)/shard_map/attend_backward/pallas_call | solution.py:178
  193.8 13.4 %attend_backward.6 = (f32[768,512]{1,0:T(8,128)S(1)}, bf16[1024,768]{1,0:T(8,128)(2,1)S(1)}, bf16[1024,768]{1,0:T(8,128)(2,1)}) custom-call(s32[2]{0:T(128)S(1)} %pad_add_fusion.1.kind_ref, bf16[512,768]{1,0:T(8,128)(2,1)S(1)} %copy-done.19, bf16[512,768]{1,0:T(8,128)(2,1)S(1)} %get-tuple-element.173.g_ref, bf16[1024,768]{1,0:T(8,128)(2,1)} %copy-done.27, ...), custom_call_target="tpu_custom_call" | custom-call | flops 8053063680 | bytes 11010048 | tf_op jit(solution)/shard_map/attend_backward/pallas_call | solution.py:178
  214.4 12.7 %attend_backward.7 = (f32[768,512]{1,0:T(8,128)}, bf16[512,768]{1,0:T(8,128)(2,1)S(1)}, bf16[512,768]{1,0:T(8,128)(2,1)S(1)}) custom-call(s32[1]{0:T(128)} %bitcast.19.kind_ref, bf16[512,768]{1,0:T(8,128)(2,1)S(1)} %copy-done.19, bf16[512,768]{1,0:T(8,128)(2,1)S(1)} %get-tuple-element.173.g_ref, bf16[512,768]{1,0:T(8,128)(2,1)S(1)} %copy-done.11, ...), custom_call_target="tpu_custom_call" | custom-call | flops 4026531840 | bytes 7864320 | tf_op jit(solution)/shard_map/attend_backward/pallas_call | solution.py:178
  243.3 4.7 convolution_convert_fusion
  286.8 14.9 %collective-permute-done.16 = bf16[512,768]{1,0:T(8,128)(2,1)S(1)} collective-permute-done((bf16[512,768]{1,0:T(8,128)(2,1)S(1)}, bf16[512,768]{1,0:T(8,128)(2,1)S(1)}, u32[]{:S(2)}, u32[]{:S(2)}) %collective-permute-start.16) | collective-permute-done | bytes 786464 | tf_op jit(solution)/shard_map/ppermute | solution.py:445
  304.5 10.9 %collective-permute-done.21 = bf16[96,2304]{1,0:T(8,128)(2,1)S(1)} collective-permute-done((bf16[96,2304]{1,0:T(8,128)(2,1)S(1)}, bf16[96,2304]{1,0:T(8,128)(2,1)S(1)}, u32[]{:S(2)}, u32[]{:S(2)}) %collective-permute-start.21) | collective-permute-done | bytes 442400 | tf_op jit(solution)/shard_map/ppermute | solution.py:250
  321.8 4.3 collective-permute-start.24
  352.7 12.2 %collective-permute-done.29 = bf16[48,2304]{1,0:T(8,128)(2,1)S(1)} collective-permute-done((bf16[48,2304]{1,0:T(8,128)(2,1)S(1)}, bf16[48,2304]{1,0:T(8,128)(2,1)S(1)}, u32[]{:S(2)}, u32[]{:S(2)}) %collective-permute-start.29) | collective-permute-done | bytes 221216 | tf_op jit(solution)/shard_map/ppermute | solution.py:250
  372.6 5.3 %collective-permute-done.58 = bf16[192,768]{1,0:T(8,128)(2,1)S(1)} collective-permute-done((bf16[192,768]{1,0:T(8,128)(2,1)S(1)}, bf16[192,768]{1,0:T(8,128)(2,1)S(1)}, u32[]{:S(2)}, u32[]{:S(2)}) %collective-permute-start.58) | collective-permute-done | bytes 294944 | tf_op jit(solution)/shard_map/ppermute | solution.py:250
  385.9 6.9 %collective-permute-start.37 = (f32[9216]{0:T(1024)S(1)}, f32[9216]{0:T(1024)S(1)}, u32[]{:S(2)}, u32[]{:S(2)}) collective-permute-start(f32[9216]{0:T(1024)S(1)} %add.544), channel_id=1, source_target_pairs={{0,1},{1,2},{2,3},{3,0},{4,5},{5,6},{6,7},{7,4},{8,9},{9,10},{10,1... | collective-permute-start | bytes 110600 | tf_op jit(solution)/shard_map/ppermute | solution.py:276
  395.7 5.5 %collective-permute-done.64 = bf16[192,384]{1,0:T(8,128)(2,1)S(1)} collective-permute-done((bf16[192,384]{1,0:T(8,128)(2,1)S(1)}, bf16[192,384]{1,0:T(8,128)(2,1)S(1)}, u32[]{:S(2)}, u32[]{:S(2)}) %collective-permute-start.64) | collective-permute-done | bytes 147488 | tf_op jit(solution)/shard_map/ppermute | solution.py:276
  403.8 4.3 collective-permute-done.66
  418.0 6.5 %collective-permute-done.44 = bf16[48,3840]{1,0:T(8,128)(2,1)S(1)} collective-permute-done((bf16[48,3840]{1,0:T(8,128)(2,1)S(1)}, bf16[48,3840]{1,0:T(8,128)(2,1)S(1)}, u32[]{:S(2)}, u32[]{:S(2)}) %collective-permute-start.44) | collective-permute-done | bytes 368672 | tf_op jit(solution)/shard_map/ppermute | solution.py:250
  432.6 7.1 %collective-permute-done.46 = bf16[48,1920]{1,0:T(8,128)(2,1)S(1)} collective-permute-done((bf16[48,1920]{1,0:T(8,128)(2,1)S(1)}, bf16[48,1920]{1,0:T(8,128)(2,1)S(1)}, u32[]{:S(2)}, u32[]{:S(2)}) %collective-permute-start.46) | collective-permute-done | bytes 184352 | tf_op jit(solution)/shard_map/ppermute | solution.py:276
  450.3 5.8 %collective-permute-done.49 = bf16[48,1920]{1,0:T(8,128)(2,1)S(1)} collective-permute-done((bf16[48,1920]{1,0:T(8,128)(2,1)S(1)}, bf16[48,1920]{1,0:T(8,128)(2,1)S(1)}, u32[]{:S(2)}, u32[]{:S(2)}) %collective-permute-start.49) | collective-permute-done | bytes 184352 | tf_op jit(solution)/shard_map/ppermute | solution.py:276
  456.1 7.3 %collective-permute-done.50 = bf16[48,1920]{1,0:T(8,128)(2,1)S(1)} collective-permute-done((bf16[48,1920]{1,0:T(8,128)(2,1)S(1)}, bf16[48,1920]{1,0:T(8,128)(2,1)S(1)}, u32[]{:S(2)}, u32[]{:S(2)}) %collective-permute-start.50) | collective-permute-done | bytes 184352 | tf_op jit(solution)/shard_map/ppermute | solution.py:276
  476.4 6.7 %collective-permute-done.54 = bf16[96,3840]{1,0:T(8,128)(2,1)S(1)} collective-permute-done((bf16[96,3840]{1,0:T(8,128)(2,1)S(1)}, bf16[96,3840]{1,0:T(8,128)(2,1)S(1)}, u32[]{:S(2)}, u32[]{:S(2)}) %collective-permute-start.54) | collective-permute-done | bytes 737312 | tf_op jit(solution)/shard_map/ppermute | solution.py:250
  494.9 13.3 %collective-permute-done.14 = bf16[512,768]{1,0:T(8,128)(2,1)S(1)} collective-permute-done((bf16[512,768]{1,0:T(8,128)(2,1)S(1)}, bf16[512,768]{1,0:T(8,128)(2,1)S(1)}, u32[]{:S(2)}, u32[]{:S(2)}) %collective-permute-start.14) | collective-permute-done | bytes 786464 | tf_op jit(solution)/shard_map/ppermute | solution.py:444
  513.5 6.4 %fusion.7 = f32[3072,768]{1,0:T(8,128)} fusion(bf16[1536,768]{1,0:T(8,128)(2,1)} %collective-permute-done.71, bf16[768,768]{1,0:T(8,128)(2,1)S(1)} %maximum_select_fusion.6, bf16[768,768]{1,0:T(8,128)(2,1)S(1)} %maximum_select_fusion.5, pred[]{:T(512)S(6)} %eq.104), kind=kLoop, calls=%fused_computation.20 | loop fusion | flops 33030144 | bytes 14155777 | tf_op jit(solution)/shard_map/convert_element_type | solution.py:300
  522.9 5.2 split.127
  (480 shorter events, 250.5 us)
Async XLA Ops:
  0.7 40.7 %collective-permute-start = (s32[512]{0:T(512)}, s32[512]{0:T(512)S(1)}, u32[]{:S(2)}, u32[]{:S(2)}) collective-permute-start(s32[512]{0:T(512)} %bitcast.135), channel_id=1, source_target_pairs={{0,1},{1,2},{2,3},{4,5},{5,6},{6,7},{8,9},{9,10},{10,11},{12,13},{... | collective-permute-start | bytes 6152 | tf_op jit(solution)/shard_map/ppermute | solution.py:350
  5.7 29.9 %collective-permute-start.3 = (s32[512]{0:T(512)}, s32[512]{0:T(512)S(1)}, u32[]{:S(2)}, u32[]{:S(2)}) collective-permute-start(s32[512]{0:T(512)} %bitcast.136), channel_id=1, source_target_pairs={{1,0},{2,1},{3,2},{5,4},{6,5},{7,6},{9,8},{10,9},{11,10},{13,12},{... | collective-permute-start | bytes 6152 | tf_op jit(solution)/shard_map/ppermute | solution.py:351
  7.0 62.7 %collective-permute-start.6 = (bf16[512,768]{1,0:T(8,128)(2,1)}, bf16[512,768]{1,0:T(8,128)(2,1)}, u32[]{:S(2)}, u32[]{:S(2)}) collective-permute-start(bf16[512,768]{1,0:T(8,128)(2,1)} %bitcast.138), channel_id=1, source_target_pairs={{0,1},{1,2},{2,3},{4,5},{5,6},{6,7},{8,9},{9,10},{10,11},{12,13},{... | collective-permute-start | bytes 2359304 | tf_op jit(solution)/shard_map/ppermute | solution.py:350
  12.5 59.2 %collective-permute-start.9 = (bf16[512,768]{1,0:T(8,128)(2,1)}, bf16[512,768]{1,0:T(8,128)(2,1)}, u32[]{:S(2)}, u32[]{:S(2)}) collective-permute-start(bf16[512,768]{1,0:T(8,128)(2,1)} %bitcast.139), channel_id=1, source_target_pairs={{1,0},{2,1},{3,2},{5,4},{6,5},{7,6},{9,8},{10,9},{11,10},{13,12},{... | collective-permute-start | bytes 2359304 | tf_op jit(solution)/shard_map/ppermute | solution.py:351
  69.7 15.6 %collective-permute-start.7 = (bf16[512,768]{1,0:T(8,128)(2,1)}, bf16[512,768]{1,0:T(8,128)(2,1)S(1)}, u32[]{:S(2)}, u32[]{:S(2)}) collective-permute-start(bf16[512,768]{1,0:T(8,128)(2,1)} %collective-permute-done.6), channel_id=1, source_target_pairs={{1,2},{2,3},{5,6},{6,7},{9,10},{10,11},{13,14},{14,15},{17,18},{18... | collective-permute-start | bytes 2359304 | tf_op jit(solution)/shard_map/ppermute | solution.py:350
  71.7 22.1 %collective-permute-start.10 = (bf16[512,768]{1,0:T(8,128)(2,1)}, bf16[512,768]{1,0:T(8,128)(2,1)S(1)}, u32[]{:S(2)}, u32[]{:S(2)}) collective-permute-start(bf16[512,768]{1,0:T(8,128)(2,1)} %collective-permute-done.9), channel_id=1, source_target_pairs={{1,0},{2,1},{5,4},{6,5},{9,8},{10,9},{13,12},{14,13},{17,16},{18,1... | collective-permute-start | bytes 2359304 | tf_op jit(solution)/shard_map/ppermute | solution.py:351
  85.3 18.5 %collective-permute-start.8 = (bf16[512,768]{1,0:T(8,128)(2,1)S(1)}, bf16[512,768]{1,0:T(8,128)(2,1)S(1)}, u32[]{:S(2)}, u32[]{:S(2)}) collective-permute-start(bf16[512,768]{1,0:T(8,128)(2,1)S(1)} %collective-permute-done.7), channel_id=1, source_target_pairs={{2,3},{6,7},{10,11},{14,15},{18,19},{22,23},{26,27},{30,31}} | collective-permute-start | bytes 2359304 | tf_op jit(solution)/shard_map/ppermute | solution.py:350
  93.8 19.6 %collective-permute-start.11 = (bf16[512,768]{1,0:T(8,128)(2,1)S(1)}, bf16[512,768]{1,0:T(8,128)(2,1)S(1)}, u32[]{:S(2)}, u32[]{:S(2)}) collective-permute-start(bf16[512,768]{1,0:T(8,128)(2,1)S(1)} %collective-permute-done.10), channel_id=1, source_target_pairs={{1,0},{5,4},{9,8},{13,12},{17,16},{21,20},{25,24},{29,28}} | collective-permute-start | bytes 2359304 | tf_op jit(solution)/shard_map/ppermute | solution.py:351
  250.9 25.9 %collective-permute-start.12 = (bf16[512,768]{1,0:T(8,128)(2,1)}, bf16[512,768]{1,0:T(8,128)(2,1)}, u32[]{:S(2)}, u32[]{:S(2)}) collective-permute-start(bf16[512,768]{1,0:T(8,128)(2,1)} %get-tuple-element.136), channel_id=1, source_target_pairs={{3,2},{7,6},{11,10},{15,14},{19,18},{23,22},{27,26},{31,30}} | collective-permute-start | bytes 2359304 | tf_op jit(solution)/shard_map/ppermute | solution.py:444
  252.5 26.2 %collective-permute-start.15 = (bf16[512,768]{1,0:T(8,128)(2,1)}, bf16[512,768]{1,0:T(8,128)(2,1)}, u32[]{:S(2)}, u32[]{:S(2)}) collective-permute-start(bf16[512,768]{1,0:T(8,128)(2,1)} %get-tuple-element.137), channel_id=1, source_target_pairs={{0,1},{4,5},{8,9},{12,13},{16,17},{20,21},{24,25},{28,29}} | collective-permute-start | bytes 2359304 | tf_op jit(solution)/shard_map/ppermute | solution.py:445
  261.9 19.9 %collective-permute-start.18 = (bf16[384,2304]{1,0:T(8,128)(2,1)}, bf16[384,2304]{1,0:T(8,128)(2,1)S(1)}, u32[]{:S(2)}, u32[]{:S(2)}) collective-permute-start(bf16[384,2304]{1,0:T(8,128)(2,1)} %constant_dynamic-slice_fusion.19), channel_id=1, source_target_pairs={{0,4},{4,0},{8,12},{12,8},{16,20},{20,16},{24,28},{28,24},{1,5},{5... | collective-permute-start | bytes 5308424 | tf_op jit(solution)/shard_map/ppermute | solution.py:250
  272.3 94.2 %collective-permute-start.40 = (bf16[384,3840]{1,0:T(8,128)(2,1)S(1)}, bf16[384,3840]{1,0:T(8,128)(2,1)}, u32[]{:S(2)}, u32[]{:S(2)}) collective-permute-start(bf16[384,3840]{1,0:T(8,128)(2,1)S(1)} %copy-done.44), channel_id=1, source_target_pairs={{0,4},{4,0},{8,12},{12,8},{16,20},{20,16},{24,28},{28,24},{1,5},{5... | collective-permute-start | bytes 8847368 | tf_op jit(solution)/shard_map/ppermute | solution.py:250
  276.8 49.4 %collective-permute-start.56 = (bf16[1536,768]{1,0:T(8,128)(2,1)S(1)}, bf16[1536,768]{1,0:T(8,128)(2,1)S(1)}, u32[]{:S(2)}, u32[]{:S(2)}) collective-permute-start(bf16[1536,768]{1,0:T(8,128)(2,1)S(1)} %constant_dynamic-slice_fusion.5), channel_id=1, source_target_pairs={{0,4},{4,0},{8,12},{12,8},{16,20},{20,16},{24,28},{28,24},{1,5},{5... | collective-permute-start | bytes 7077896 | tf_op jit(solution)/shard_map/ppermute | solution.py:250
  276.8 209.4 %collective-permute-start.39 = (f32[9216]{0:T(1024)S(1)}, f32[9216]{0:T(1024)}, u32[]{:S(2)}, u32[]{:S(2)}) collective-permute-start(f32[9216]{0:T(1024)S(1)} %add.544), channel_id=1, source_target_pairs={{0,3},{1,0},{2,1},{3,2},{4,7},{5,4},{6,5},{7,6},{8,11},{9,8},{10,9... | collective-permute-start | bytes 110600 | tf_op jit(solution)/shard_map/ppermute | solution.py:276
  281.8 19.8 %collective-permute-start.16 = (bf16[512,768]{1,0:T(8,128)(2,1)S(1)}, bf16[512,768]{1,0:T(8,128)(2,1)S(1)}, u32[]{:S(2)}, u32[]{:S(2)}) collective-permute-start(bf16[512,768]{1,0:T(8,128)(2,1)S(1)} %get-tuple-element.129), channel_id=1, source_target_pairs={{0,1},{1,2},{4,5},{5,6},{8,9},{9,10},{12,13},{13,14},{16,17},{17,1... | collective-permute-start | bytes 2359304 | tf_op jit(solution)/shard_map/ppermute | solution.py:445
  285.2 18.5 %collective-permute-start.19 = (bf16[96,2304]{1,0:T(8,128)(2,1)S(1)}, bf16[96,2304]{1,0:T(8,128)(2,1)S(1)}, u32[]{:S(2)}, u32[]{:S(2)}) collective-permute-start(bf16[96,2304]{1,0:T(8,128)(2,1)S(1)} %constant_dynamic-slice_fusion.18), channel_id=1, source_target_pairs={{0,8},{4,12},{8,0},{12,4},{16,24},{20,28},{24,16},{28,20},{1,9},{5... | collective-permute-start | bytes 1327112 | tf_op jit(solution)/shard_map/ppermute | solution.py:250
  303.9 14.6 %collective-permute-start.20 = (bf16[48,2304]{1,0:T(8,128)(2,1)S(1)}, bf16[48,2304]{1,0:T(8,128)(2,1)S(1)}, u32[]{:S(2)}, u32[]{:S(2)}) collective-permute-start(bf16[48,2304]{1,0:T(8,128)(2,1)S(1)} %constant_dynamic-slice_fusion.17), channel_id=1, source_target_pairs={{0,16},{4,20},{8,24},{12,28},{16,0},{20,4},{24,8},{28,12},{1,17},{... | collective-permute-start | bytes 663560 | tf_op jit(solution)/shard_map/ppermute | solution.py:250
  346.0 24.9 %collective-permute-start.57 = (bf16[384,768]{1,0:T(8,128)(2,1)S(1)}, bf16[384,768]{1,0:T(8,128)(2,1)S(1)}, u32[]{:S(2)}, u32[]{:S(2)}) collective-permute-start(bf16[384,768]{1,0:T(8,128)(2,1)S(1)} %constant_dynamic-slice_fusion.4), channel_id=1, source_target_pairs={{0,8},{4,12},{8,0},{12,4},{16,24},{20,28},{24,16},{28,20},{1,9},{5... | collective-permute-start | bytes 1769480 | tf_op jit(solution)/shard_map/ppermute | solution.py:250
  346.6 25.1 %collective-permute-start.59 = (bf16[384,768]{1,0:T(8,128)(2,1)S(1)}, bf16[384,768]{1,0:T(8,128)(2,1)S(1)}, u32[]{:S(2)}, u32[]{:S(2)}) collective-permute-start(bf16[384,768]{1,0:T(8,128)(2,1)S(1)} %constant_dynamic-slice_fusion.2), channel_id=1, source_target_pairs={{0,16},{4,20},{8,24},{12,28},{16,0},{20,4},{24,8},{28,12},{1,17},{... | collective-permute-start | bytes 1769480 | tf_op jit(solution)/shard_map/ppermute | solution.py:250
  351.1 13.8 %collective-permute-start.29 = (bf16[48,2304]{1,0:T(8,128)(2,1)S(1)}, bf16[48,2304]{1,0:T(8,128)(2,1)S(1)}, u32[]{:S(2)}, u32[]{:S(2)}) collective-permute-start(bf16[48,2304]{1,0:T(8,128)(2,1)S(1)} %get-tuple-element.134), channel_id=1, source_target_pairs={{0,16},{4,20},{8,24},{12,28},{16,0},{20,4},{24,8},{28,12},{1,17},{... | collective-permute-start | bytes 663560 | tf_op jit(solution)/shard_map/ppermute | solution.py:250
  364.9 16.4 %collective-permute-start.32 = (bf16[96,2304]{1,0:T(8,128)(2,1)S(1)}, bf16[96,2304]{1,0:T(8,128)(2,1)S(1)}, u32[]{:S(2)}, u32[]{:S(2)}) collective-permute-start(bf16[96,2304]{1,0:T(8,128)(2,1)S(1)} %maximum_select_fusion.14), channel_id=1, source_target_pairs={{0,16},{4,20},{8,24},{12,28},{16,0},{20,4},{24,8},{28,12},{1,17},{... | collective-permute-start | bytes 1327112 | tf_op jit(solution)/shard_map/ppermute | solution.py:250
  366.5 28.0 %collective-permute-start.30 = (bf16[96,2304]{1,0:T(8,128)(2,1)S(1)}, bf16[96,2304]{1,0:T(8,128)(2,1)S(1)}, u32[]{:S(2)}, u32[]{:S(2)}) collective-permute-start(bf16[96,2304]{1,0:T(8,128)(2,1)S(1)} %maximum_select_fusion.13), channel_id=1, source_target_pairs={{0,8},{4,12},{8,0},{12,4},{16,24},{20,28},{24,16},{28,20},{1,9},{5... | collective-permute-start | bytes 1327112 | tf_op jit(solution)/shard_map/ppermute | solution.py:250
  380.1 13.7 %collective-permute-start.62 = (bf16[192,384]{1,0:T(8,128)(2,1)S(1)}, bf16[192,384]{1,0:T(8,128)(2,1)S(1)}, u32[]{:S(2)}, u32[]{:S(2)}) collective-permute-start(bf16[192,384]{1,0:T(8,128)(2,1)S(1)} %get-tuple-element.142), channel_id=1, source_target_pairs={{0,2},{1,3},{2,0},{3,1},{4,6},{5,7},{6,4},{7,5},{8,10},{9,11},{10,... | collective-permute-start | bytes 442376 | tf_op jit(solution)/shard_map/ppermute | solution.py:276
  385.9 102.0 %collective-permute-start.37 = (f32[9216]{0:T(1024)S(1)}, f32[9216]{0:T(1024)S(1)}, u32[]{:S(2)}, u32[]{:S(2)}) collective-permute-start(f32[9216]{0:T(1024)S(1)} %add.544), channel_id=1, source_target_pairs={{0,1},{1,2},{2,3},{3,0},{4,5},{5,6},{6,7},{7,4},{8,9},{9,10},{10,1... | collective-permute-start | bytes 110600 | tf_op jit(solution)/shard_map/ppermute | solution.py:276
  393.8 14.4 %collective-permute-start.41 = (bf16[96,3840]{1,0:T(8,128)(2,1)S(1)}, bf16[96,3840]{1,0:T(8,128)(2,1)S(1)}, u32[]{:S(2)}, u32[]{:S(2)}) collective-permute-start(bf16[96,3840]{1,0:T(8,128)(2,1)S(1)} %constant_dynamic-slice_fusion.11), channel_id=1, source_target_pairs={{0,8},{4,12},{8,0},{12,4},{16,24},{20,28},{24,16},{28,20},{1,9},{5... | collective-permute-start | bytes 2211848 | tf_op jit(solution)/shard_map/ppermute | solution.py:250
  442.8 21.7 %collective-permute-start.70 = (bf16[384,768]{1,0:T(8,128)(2,1)S(1)}, bf16[384,768]{1,0:T(8,128)(2,1)S(1)}, u32[]{:S(2)}, u32[]{:S(2)}) collective-permute-start(bf16[384,768]{1,0:T(8,128)(2,1)S(1)} %maximum_select_fusion.12), channel_id=1, source_target_pairs={{0,16},{4,20},{8,24},{12,28},{16,0},{20,4},{24,8},{28,12},{1,17},{... | collective-permute-start | bytes 1769480 | tf_op jit(solution)/shard_map/ppermute | solution.py:250
  446.6 18.4 %collective-permute-start.68 = (bf16[384,768]{1,0:T(8,128)(2,1)S(1)}, bf16[384,768]{1,0:T(8,128)(2,1)S(1)}, u32[]{:S(2)}, u32[]{:S(2)}) collective-permute-start(bf16[384,768]{1,0:T(8,128)(2,1)S(1)} %maximum_select_fusion.11), channel_id=1, source_target_pairs={{0,8},{4,12},{8,0},{12,4},{16,24},{20,28},{24,16},{28,20},{1,9},{5... | collective-permute-start | bytes 1769480 | tf_op jit(solution)/shard_map/ppermute | solution.py:250
  464.5 24.0 %collective-permute-start.38 = (f32[9216]{0:T(1024)S(1)}, f32[9216]{0:T(1024)S(1)}, u32[]{:S(2)}, u32[]{:S(2)}) collective-permute-start(f32[9216]{0:T(1024)S(1)} %add.544), channel_id=1, source_target_pairs={{0,2},{1,3},{2,0},{3,1},{4,6},{5,7},{6,4},{7,5},{8,10},{9,11},{10,... | collective-permute-start | bytes 110600 | tf_op jit(solution)/shard_map/ppermute | solution.py:276
  485.7 23.9 %collective-permute-start.33 = (bf16[384,2304]{1,0:T(8,128)(2,1)S(1)}, bf16[384,2304]{1,0:T(8,128)(2,1)S(1)}, u32[]{:S(2)}, u32[]{:S(2)}) collective-permute-start(bf16[384,2304]{1,0:T(8,128)(2,1)S(1)} %pad_maximum_fusion.3), channel_id=1, source_target_pairs={{0,4},{4,0},{8,12},{12,8},{16,20},{20,16},{24,28},{28,24},{1,5},{5... | collective-permute-start | bytes 5308424 | tf_op jit(solution)/shard_map/ppermute | solution.py:250
  486.2 22.0 %collective-permute-start.14 = (bf16[512,768]{1,0:T(8,128)(2,1)S(1)}, bf16[512,768]{1,0:T(8,128)(2,1)S(1)}, u32[]{:S(2)}, u32[]{:S(2)}) collective-permute-start(bf16[512,768]{1,0:T(8,128)(2,1)S(1)} %get-tuple-element.119), channel_id=1, source_target_pairs={{1,0},{2,1},{3,2},{5,4},{6,5},{7,6},{9,8},{10,9},{11,10},{13,12},{... | collective-permute-start | bytes 2359304 | tf_op jit(solution)/shard_map/ppermute | solution.py:444
  487.9 25.6 %collective-permute-start.71 = (bf16[1536,768]{1,0:T(8,128)(2,1)}, bf16[1536,768]{1,0:T(8,128)(2,1)}, u32[]{:S(2)}, u32[]{:S(2)}) collective-permute-start(bf16[1536,768]{1,0:T(8,128)(2,1)} %pad_maximum_fusion.2), channel_id=1, source_target_pairs={{0,4},{4,0},{8,12},{12,8},{16,20},{20,16},{24,28},{28,24},{1,5},{5... | collective-permute-start | bytes 7077896 | tf_op jit(solution)/shard_map/ppermute | solution.py:250
  488.5 31.5 %collective-permute-start.55 = (bf16[384,3840]{1,0:T(8,128)(2,1)S(1)}, bf16[384,3840]{1,0:T(8,128)(2,1)S(1)}, u32[]{:S(2)}, u32[]{:S(2)}) collective-permute-start(bf16[384,3840]{1,0:T(8,128)(2,1)S(1)} %pad_maximum_fusion.1), channel_id=1, source_target_pairs={{0,4},{4,0},{8,12},{12,8},{16,20},{20,16},{24,28},{28,24},{1,5},{5... | collective-permute-start | bytes 8847368 | tf_op jit(solution)/shard_map/ppermute | solution.py:250
  (128 other events, 772.4 us)

commit v2 on v0

v2 whole, which is shorter than its diff:
```python
import functools

import jax
import jax.numpy as jnp
from jax import lax
from jax.experimental import pallas as pl
from jax.experimental.pallas import tpu as pltpu
from jax.sharding import PartitionSpec as P

HEAD_DIM = 64
PAIR = 2 * HEAD_DIM
MASKED = -1e30
EPSILON = 1e-05
ROOT_HALF = 0.7071067811865476
ROOT_TAU = 0.3989422804014327
PHASES = 1
ID_BASE = 128

NT = (((1,), (1,)), ((), ()))
NN = (((1,), (0,)), ((), ()))
TN = (((0,), (0,)), ((), ()))


def dot(left, right, dims):
    return lax.dot_general(left, right, dims, preferred_element_type=jnp.float32)


def low(x):
    return x.astype(jnp.bfloat16)


def high(x):
    return x.astype(jnp.float32)


def times(left, right):
    return dot(left, right, NN)


def times_back(left, right):
    return dot(left, right, NT)


def weight_grad(left, right):
    return dot(left, right, TN)


def column_sums(x):
    return jnp.sum(high(x), axis=0)


def lane_half(x, half):
    lanes = lax.broadcasted_iota(jnp.int32, x.shape, 1)
    keep = lanes < HEAD_DIM if half == 0 else lanes >= HEAD_DIM
    return jnp.where(keep, x, jnp.zeros_like(x))


def head_rows(half):
    return slice(half * HEAD_DIM, (half + 1) * HEAD_DIM)


def look(kind_ref, bias_ref, ids_q_ref, ids_k_ref):
    @pl.when(pl.program_id(0) == 0)
    def _():
        ids_q, ids_k = ids_q_ref[...], ids_k_ref[...]
        low_q, high_q, low_k, high_k = jnp.min(ids_q), jnp.max(ids_q), jnp.min(ids_k), jnp.max(ids_k)
        apart = (high_q < low_k) | (high_k < low_q)
        one = (low_q == high_k) & (low_k == high_q)
        kind_ref[0] = jnp.where(apart, 0, jnp.where(one, 1, 2)).astype(jnp.int32)

        @pl.when(kind_ref[0] == 2)
        def _():
            bias_ref[...] = jnp.where(ids_k == ids_q, 0.0, MASKED)


def forward_kernel(first, last, q_ref, k_ref, v_ref, ids_q_ref, ids_k_ref, *refs):
    if first:
        acc_in = peak_in = sum_in = None
    else:
        acc_in, peak_in, sum_in = refs[:3]
        refs = refs[3:]
    if last:
        acc_out, total_out, attended_out, acc, peak, sums, kind_ref, bias_ref = refs
    else:
        acc, peak, sums, kind_ref, bias_ref = refs
    if first:
        acc[...] = jnp.zeros_like(acc)
        sums[...] = jnp.zeros_like(sums)
        peak[...] = jnp.full(peak.shape, MASKED, jnp.float32)
    else:
        acc[...] = acc_in[...]
        sums[...] = sum_in[...]
        peak[...] = peak_in[...]
    look(kind_ref, bias_ref, ids_q_ref, ids_k_ref)

    def visit(masked):
        q, k = q_ref[...], k_ref[...]
        v_t = v_ref[...].T
        ones = jnp.ones((16, k.shape[0]), jnp.bfloat16)
        scores = [dot(k, lane_half(q, half), NT) for half in range(2)]
        if masked:
            scores = [x + bias_ref[...] for x in scores]
        old = [peak[0, half : half + 1, :] for half in range(2)]
        new = [jnp.maximum(o, jnp.max(x, axis=0, keepdims=True)) for o, x in zip(old, scores)]
        prob = [low(jnp.exp(x - m)) for x, m in zip(scores, new)]
        for half in range(2):
            shrink = jnp.exp(old[half] - new[half])
            rows, one = head_rows(half), slice(half, half + 1)
            mixed = dot(jnp.concatenate([v_t[rows], ones], axis=0), prob[half], NN)
            acc[rows, :] = acc[rows, :] * shrink + mixed[:HEAD_DIM]
            sums[0, one, :] = sums[0, one, :] * shrink + mixed[HEAD_DIM : HEAD_DIM + 1]
            peak[0, one, :] = new[half]

    pl.when(kind_ref[0] == 1)(functools.partial(visit, False))
    pl.when(kind_ref[0] == 2)(functools.partial(visit, True))

    if last:
        for half in range(2):
            rows, one = head_rows(half), slice(half, half + 1)
            acc_out[rows, :] = acc[rows, :] / sums[0, one, :]
            total_out[0, one, :] = peak[0, one, :] + jnp.log(sums[0, one, :])
        attended_out[...] = low(acc_out[...].T)


def attend_forward(q, kv, ids_q, ids_k, state, last):
    block, width = q.shape
    pairs = width // PAIR
    first = state is None
    rows = pl.BlockSpec((1, 2, block), lambda p: (p, 0, 0))
    acc = pl.BlockSpec((PAIR, block), lambda p: (p, 0))
    mine = pl.BlockSpec((block, PAIR), lambda p: (0, p))
    acc_shape = jax.ShapeDtypeStruct((width, block), jnp.float32)
    row_shape = jax.ShapeDtypeStruct((pairs, 2, block), jnp.float32)
    scratch = [pltpu.SMEM((1,), jnp.int32), pltpu.VMEM((block, block), jnp.float32)]
    if last:
        out_specs = [acc, rows, mine]
        out_shape = [acc_shape, row_shape, jax.ShapeDtypeStruct((block, width), jnp.bfloat16)]
        scratch = [
            pltpu.VMEM((PAIR, block), jnp.float32),
            pltpu.VMEM((1, 2, block), jnp.float32),
            pltpu.VMEM((1, 2, block), jnp.float32),
        ] + scratch
    else:
        out_specs, out_shape = [acc, rows, rows], [acc_shape, row_shape, row_shape]
    return pl.pallas_call(
        functools.partial(forward_kernel, first, last),
        grid_spec=pl.GridSpec(
            grid=(pairs,),
            in_specs=[
                mine,
                mine,
                pl.BlockSpec((block, PAIR), lambda p: (0, p + pairs)),
                pl.BlockSpec((1, block), lambda p: (0, 0)),
                pl.BlockSpec((block, 1), lambda p: (0, 0)),
            ]
            + ([] if first else [acc, rows, rows]),
            out_specs=out_specs,
            scratch_shapes=scratch,
        ),
        out_shape=out_shape,
        compiler_params=pltpu.CompilerParams(vmem_limit_bytes=32 * 2**20),
        cost_estimate=pl.CostEstimate(
            flops=block, bytes_accessed=block, transcendentals=0
        ),
        name="attend_forward",
    )(q, kv, kv, ids_q, ids_k, *([] if first else state))


def backward_kernel(
    first, last, pairs, q_ref, g_ref, k_ref, v_ref, o_ref, total_ref, ids_q_ref, ids_k_ref, *refs
):
    if not first:
        grad_q_in, refs = refs[0], refs[1:]
    grad_kv, sums, grad_q_out, grad_q, kind_ref, bias_ref = refs if last else refs[:2] + (None,) + refs[2:]
    if first:
        grad_q[...] = jnp.zeros_like(grad_q)
    else:
        grad_q[...] = grad_q_in[...]
    look(kind_ref, bias_ref, ids_q_ref, ids_k_ref)
    step = pl.program_id(0)
    k_columns = pl.ds(pl.multiple_of(step * PAIR, PAIR), PAIR)
    v_columns = pl.ds(pl.multiple_of((step + pairs) * PAIR, PAIR), PAIR)

    def visit(masked):
        q, g, k, v = q_ref[...], g_ref[...], k_ref[...], v_ref[...]
        k_t = k.T
        products = high(g).T * o_ref[...]
        sum_k = sum_v = None
        for half in range(2):
            rows = head_rows(half)
            q_half, g_half = lane_half(q, half), lane_half(g, half)
            delta = jnp.sum(products[rows], axis=0, keepdims=True)
            scores = dot(k, q_half, NT)
            if masked:
                scores = scores + bias_ref[...]
            prob = jnp.exp(scores - total_ref[0, half : half + 1, :])
            grad_prob = dot(v, g_half, NT)
            grad_score = low(prob * (grad_prob - delta))
            part_v = dot(low(prob), g_half, NN)
            part_k = dot(grad_score, q_half, NN)
            sum_v = part_v if sum_v is None else sum_v + part_v
            sum_k = part_k if sum_k is None else sum_k + part_k
            grad_q[rows, :] += dot(k_t[rows], grad_score, NN)
        grad_kv[:, k_columns] = low(sum_k)
        grad_kv[:, v_columns] = low(sum_v)
        sums[0:1, k_columns] = jnp.sum(high(low(sum_v)), axis=0, keepdims=True)

    pl.when(kind_ref[0] == 1)(functools.partial(visit, False))
    pl.when(kind_ref[0] == 2)(functools.partial(visit, True))

    @pl.when(kind_ref[0] == 0)
    def _():
        nothing = jnp.zeros((grad_kv.shape[0], PAIR), jnp.bfloat16)
        grad_kv[:, k_columns] = nothing
        grad_kv[:, v_columns] = nothing
        sums[0:1, k_columns] = jnp.zeros((1, PAIR), jnp.float32)

    if last:
        grad_queries = low(grad_q[...].T * HEAD_DIM ** (-0.5))
        grad_q_out[...] = grad_queries
        sums[1:2, k_columns] = jnp.sum(high(grad_queries), axis=0, keepdims=True)


def attend_backward(phase, q, g, kv, attended_t, totals, ids_q, ids_k, grad_q, last):
    block, width = q.shape
    all_pairs = width // PAIR
    pairs = all_pairs // PHASES
    offset = phase * pairs
    first = grad_q is None
    mine = pl.BlockSpec((block, PAIR), lambda p: (0, p + offset))
    acc = pl.BlockSpec((PAIR, block), lambda p: (p, 0))
    out_specs = [
        pl.BlockSpec((block, 2 * pairs * PAIR), lambda p: (0, 0)),
        pl.BlockSpec((2, pairs * PAIR), lambda p: (0, 0)),
    ]
    out_shape = [
        jax.ShapeDtypeStruct((block, 2 * pairs * PAIR), jnp.bfloat16),
        jax.ShapeDtypeStruct((2, pairs * PAIR), jnp.float32),
    ]
    scratch = [pltpu.SMEM((1,), jnp.int32), pltpu.VMEM((block, block), jnp.float32)]
    if last:
        out_specs += [pl.BlockSpec((block, PAIR), lambda p: (0, p))]
        out_shape += [jax.ShapeDtypeStruct((block, pairs * PAIR), jnp.bfloat16)]
        scratch = [pltpu.VMEM((PAIR, block), jnp.float32)] + scratch
    else:
        out_specs += [acc]
        out_shape += [jax.ShapeDtypeStruct((pairs * PAIR, block), jnp.float32)]
    return pl.pallas_call(
        functools.partial(backward_kernel, first, last, pairs),
        grid_spec=pl.GridSpec(
            grid=(pairs,),
            in_specs=[
                mine,
                mine,
                mine,
                pl.BlockSpec((block, PAIR), lambda p: (0, p + offset + all_pairs)),
                pl.BlockSpec((PAIR, block), lambda p: (p + offset, 0)),
                pl.BlockSpec((1, 2, block), lambda p: (p + offset, 0, 0)),
                pl.BlockSpec((1, block), lambda p: (0, 0)),
                pl.BlockSpec((block, 1), lambda p: (0, 0)),
            ]
            + ([] if first else [acc]),
            out_specs=out_specs,
            scratch_shapes=scratch,
        ),
        out_shape=out_shape,
        compiler_params=pltpu.CompilerParams(vmem_limit_bytes=32 * 2**20),
        cost_estimate=pl.CostEstimate(
            flops=block, bytes_accessed=block, transcendentals=0
        ),
        name="attend_backward",
    )(q, g, kv, kv, attended_t, totals, ids_q, ids_k, *([] if first else [grad_q]))


def layer_norm(values, gain, shift):
    center = values - jnp.mean(values, axis=-1, keepdims=True)
    inverse = lax.rsqrt(jnp.mean(center * center, axis=-1, keepdims=True) + EPSILON)
    scaled = center * inverse
    return scaled * gain + shift, scaled, inverse


def norm_back(grad_out, scaled, inverse, gain):
    grad_scaled = grad_out * gain
    grad_in = inverse * (
        grad_scaled
        - jnp.mean(grad_scaled, axis=-1, keepdims=True)
        - scaled * jnp.mean(grad_scaled * scaled, axis=-1, keepdims=True)
    )
    return grad_in, jnp.sum(grad_out * scaled, axis=0), jnp.sum(grad_out, axis=0)


def pick(x, index, parts):
    size = x.shape[0] // parts
    return lax.dynamic_slice_in_dim(x, index * size, size, 0)


def add_low(left, right):
    return low(high(left) + high(right))


def steps_of(batch, seq):
    chips = [1 << i for i in range(1, batch.bit_length() - 1)]
    places = [1 << i for i in range(seq.bit_length() - 1)]
    return [("batch", 1, 1), *(("batch", a, b) for a, b in zip(chips, chips[::-1])), *(("seq", p, p) for p in places)]


def partner(x, step, counts):
    axis, even, odd = step
    if axis == "seq":
        paths = [(i, i ^ even) for i in range(counts["seq"])]
    else:
        paths = [(i, i ^ (odd if i % 2 else even)) for i in range(counts["batch"])]
    return x, lambda x: lax.ppermute(x, axis, paths)


def side_of(step):
    axis, even, odd = step
    index = lax.axis_index(axis)
    if even == odd:
        return (index // even) % 2
    return jnp.where(lax.axis_index("batch") % 2 == 0, (index // even) % 2, (index // odd) % 2)


def join(x, other, side):
    return jnp.where(side == 0, jnp.concatenate([x, other], axis=0), jnp.concatenate([other, x], axis=0))


def passed(x, step, counts):
    x, call = partner(x, step, counts)
    return call(x)


def down(x, step, counts):
    side = side_of(step)
    return add_low(pick(x, side, 2), passed(pick(x, 1 - side, 2), step, counts))


def up(x, step, counts):
    return join(x, passed(x, step, counts), side_of(step))


def up_last(x, step, counts, cuts):
    got = passed(x, step, counts)
    edges = [0, *cuts, x.shape[1]]
    return [high(join(x[:, a:b], got[:, a:b], side_of(step))) for a, b in zip(edges[:-1], edges[1:])]


def apart(certain, run):
    shapes = jax.eval_shape(run)
    return lax.cond(certain, run, lambda: jax.tree.map(lambda x: jnp.zeros(x.shape, x.dtype), shapes))


def visits(me, seq):
    short, long = (("L", me), ("R", seq - 1 - me))
    if short[1] > long[1]:
        short, long = long, short
    order = []
    for k in range(1, short[1] + 1):
        order += [(short[0], k), (long[0], k)]
    return order + [(long[0], k) for k in range(short[1] + 1, long[1] + 1)]


def choose(me, options):
    known = [(i, x) for i, x in enumerate(options) if x is not None]
    value = known[-1][1]
    for i, x in reversed(known[:-1]):
        if x is not value:
            value = jnp.where(me == i, x, value)
    return value


def pack_ids(ids, width):
    whole = jnp.zeros((8, width), jnp.bfloat16)
    both = jnp.stack([ids // ID_BASE, ids % ID_BASE]).astype(jnp.bfloat16)
    return lax.dynamic_update_slice(whole, both, (0, 0))


def unpack_ids(rows, block):
    rows = rows[:, :block].astype(jnp.int32)
    return rows[0] * ID_BASE + rows[1]


def shards(
    batch,
    seq,
    hidden_in,
    document_ids,
    query_weight,
    query_bias,
    key_weight,
    value_weight,
    value_bias,
    proj_weight,
    proj_bias,
    first_gain,
    first_shift,
    inner_weight,
    inner_bias,
    outer_weight,
    outer_bias,
    second_gain,
    second_shift,
    output_grad,
):
    hidden = hidden_in[0]
    ids = document_ids[0]
    block, width = hidden.shape
    half = width // PHASES
    me = lax.axis_index("seq")
    counts = {"batch": batch, "seq": seq}

    orders = [visits(i, seq) for i in range(seq)]

    came = {("L", 0): jnp.concatenate([hidden, pack_ids(ids, width)], axis=0)}
    came["R", 0] = came["L", 0]

    kv_weight = jnp.concatenate([key_weight, value_weight], axis=1)
    kv_bias = jnp.concatenate([jnp.zeros_like(value_bias), value_bias])
    queries = low(times(hidden, query_weight) + query_bias) * jnp.bfloat16(HEAD_DIM ** (-0.5))
    ids_q = ids[None, :]
    state = None
    kept = []
    for s in range(seq):
        if s < seq - 1:
            to_right = lax.ppermute(came["L", s], "seq", [(i, i + 1) for i in range(s, seq - 1)])
            to_left = lax.ppermute(came["R", s], "seq", [(i, i - 1) for i in range(1, seq - s)])
        if s == 0:
            packed, ids_k = came["L", 0], ids
        else:
            packed = choose(me, [came[orders[i][s - 1]] for i in range(seq)])
            ids_k = unpack_ids(packed[block:], block)
        tokens = hidden if s == 0 else packed[:block]
        kv = low(times(tokens, kv_weight) + kv_bias)
        state = attend_forward(queries, kv, ids_q, ids_k[:, None], state, s == seq - 1)
        if s < seq - 1:
            came["L", s + 1], came["R", s + 1], state = lax.optimization_barrier((to_right, to_left, state))
        kept.append((hidden if s == 0 else packed, kv, ids_k[:, None]))
    attended_t, totals, attended = state

    branch = times(attended, proj_weight) + proj_bias
    first, first_scaled, first_inverse = layer_norm(high(hidden) + branch, first_gain, first_shift)
    first_low = low(first)
    inner_act = times(first_low, inner_weight) + inner_bias
    chance = 0.5 * (1.0 + lax.erf(inner_act * ROOT_HALF))
    activated = low(inner_act * chance)
    slope = low(chance + inner_act * (ROOT_TAU * jnp.exp(-0.5 * inner_act * inner_act)))
    activated, slope = lax.optimization_barrier((activated, slope))
    outer_act = times(activated, outer_weight) + outer_bias
    second, second_scaled, second_inverse = layer_norm(first + outer_act, second_gain, second_shift)
    result = low(second)
    grad_mix, grad_second_gain, grad_second_shift = norm_back(
        high(output_grad[0]), second_scaled, second_inverse, second_gain
    )
    grad_outer = low(grad_mix)
    grad_outer_bias = column_sums(grad_outer)
    grad_inner = low(times_back(grad_outer, outer_weight) * high(slope))
    early = (low(weight_grad(activated, grad_outer)), low(weight_grad(first_low, grad_inner)))
    early, grad_inner = lax.optimization_barrier((early, grad_inner))
    early_sums = lax.psum(early, ("batch", "seq"))

    certain = ids[0] >= 0
    steps = steps_of(**counts)
    far = len(steps) - 1

    def attention_part():
        grad_inner_bias = column_sums(grad_inner)
        grad_first = grad_mix + times_back(grad_inner, inner_weight)
        grad_resid, grad_first_gain, grad_first_shift = norm_back(
            grad_first, first_scaled, first_inverse, first_gain
        )
        grad_branch = low(grad_resid)
        grad_attended = low(times_back(grad_branch, proj_weight))
        grad_query = None
        kv_grad = 0.0
        grad_value_bias = 0.0
        terms = {}
        for s in reversed(range(seq)):
            packed, kv, ids_k = kept[s]
            grad_kv, sums, grad_query = attend_backward(
                0, queries, grad_attended, kv, attended_t, totals, ids_q, ids_k, grad_query, s == 0
            )
            kv_grad += weight_grad(packed[:block], grad_kv)
            grad_value_bias += sums[0]
            terms[s] = low(times_back(grad_kv, kv_weight))
        late = jnp.concatenate(
            [low(weight_grad(hidden, grad_query)), low(kv_grad), low(weight_grad(attended, grad_branch))], axis=1
        )
        vectors = jnp.stack(
            [
                sums[1],
                grad_value_bias,
                column_sums(grad_branch),
                grad_first_gain,
                grad_first_shift,
                grad_outer_bias,
                grad_second_gain,
                grad_second_shift,
                *jnp.split(grad_inner_bias, inner_weight.shape[1] // width),
            ]
        )
        own_terms = grad_resid + high(terms[0]) + times_back(grad_query, query_weight)
        vectors = vectors + passed(vectors, steps[0], counts)
        return down(late, steps[0], counts), vectors, own_terms, [terms[s] for s in range(1, seq)]

    late, sums, own_terms, terms = apart(certain, attention_part)
    terms = dict(enumerate(terms, 1))

    def homeward(s):
        found = []
        for side in "LR":
            options = [terms[orders[i].index((side, s)) + 1] if (side, s) in orders[i] else None for i in range(seq)]
            found.append(choose(me, options))
        return found

    def send(s, sends):
        return [
            lax.ppermute(sends[0], "seq", [(i, i - 1) for i in range(s, seq)]),
            lax.ppermute(sends[1], "seq", [(i, i + 1) for i in range(seq - s)]),
        ]

    chips = [i for i, step in enumerate(steps) if i > 0 and step[0] == "batch"]
    places = [i for i, step in enumerate(steps) if step[0] == "seq"]

    def down_chips(late, sums):
        for i in chips:
            sums = sums + passed(sums, steps[i], counts)
            late = down(late, steps[i], counts)
        return late, sums, {s: homeward(s) for s in range(1, seq - 1)}

    def along_row(late, sums):
        for i in places:
            sums = sums + passed(sums, steps[i], counts)
            late = down(late, steps[i], counts)
        for i in places[::-1]:
            late = up(late, steps[i], counts)
        return late, sums

    late, on_way = lax.optimization_barrier((late, homeward(seq - 1)))
    on_way = send(seq - 1, on_way)
    late, sums, found = apart(certain, functools.partial(down_chips, late, sums))
    on_way, late, sums = lax.optimization_barrier((on_way, late, sums))
    late, sums = apart(certain, functools.partial(along_row, late, sums))
    work = [functools.partial(lambda i, x: up(x, steps[i], counts), i) for i in chips[::-1]]
    for s in reversed(range(1, seq - 1)):
        totals_home = [low(high(x) + high(o)) for x, o in zip(found[s], on_way)]
        late, totals_home = lax.optimization_barrier((late, totals_home))
        on_way = send(s, totals_home)
        if s == seq - 2:
            for i, run in enumerate(work):
                if i == len(work) - 1:
                    late, early_sums = apart(
                        certain, lambda x=late: (run(x), [high(y) for y in early_sums])
                    )
                else:
                    late = apart(certain, functools.partial(run, late))
                late, early_sums = lax.optimization_barrier((late, early_sums))
            on_way, late = lax.optimization_barrier((on_way, late))
    late = apart(
        certain, lambda: up_last(late, steps[0], counts, (width, 2 * width, 3 * width))
    )
    vectors = sums
    grad_query_weight, grad_key_weight, grad_value_weight, grad_proj_weight = late
    grad_input = low(own_terms + high(on_way[0]) + high(on_way[1]))
    grad_outer_weight, grad_inner_weight = early_sums
    (
        grad_query_bias,
        grad_value_bias,
        grad_proj_bias,
        grad_first_gain,
        grad_first_shift,
        grad_outer_bias,
        grad_second_gain,
        grad_second_shift,
    ) = (vectors[i] for i in range(8))
    grad_inner_bias = vectors[8:].reshape(-1)
    return (
        result[None],
        grad_input[None],
        grad_query_weight,
        grad_query_bias,
        grad_key_weight,
        grad_value_weight,
        grad_value_bias,
        grad_proj_weight,
        grad_proj_bias,
        grad_first_gain,
        grad_first_shift,
        grad_inner_weight,
        grad_inner_bias,
        grad_outer_weight,
        grad_outer_bias,
        grad_second_gain,
        grad_second_shift,
    )


def solution(mesh):
    rows = P("batch", "seq", None)
    return jax.shard_map(
        functools.partial(shards, mesh.shape["batch"], mesh.shape["seq"]),
        mesh=mesh,
        in_specs=(rows, P("batch", "seq")) + (P(),) * 15 + (rows,),
        out_specs=(rows, rows) + (P(),) * 15,
        check_vma=False,
    )
```

time: 997 us -> 402 us (0.40)
  the two profiles are of different devices: /device:TPU:0 before, /device:TPU:26 now
where the time goes in v2:
time: 402 us; the launch traced here: 395 us
  waiting for transfers between devices  109 us (27%)
  Pallas kernels  74 us (18%)
  other arithmetic  66.6 us (17%)
  matrix products  64.8 us (16%)
  starting transfers between devices  41.7 us (10%)
  local copies, waits for them, and re-layouts  21.9 us (5%)
  between operations  15.9 us (4%)
    ppermute x15, waiting for transfers between devices, partner(): return (x, lambda x: lax.ppermute(x, axis, paths))  84.2 us
    dot_general x24, matrix products, dot(): lax.dot_general(left, right, dims, preferred_element_type=jnp.float32)  64.8 us
    pallas_call x4, Pallas kernels, attend_backward(): pl.pallas_call(functools.partial(backward_kernel, first, last, pairs), gr...  44.5 us
    pallas_call x4, Pallas kernels, attend_forward(): pl.pallas_call(functools.partial(forward_kernel, first, last), grid_spec=...  29.5 us
    convert_element_type x7, other arithmetic, high(): return x.astype(jnp.float32)  24.9 us
    convert_element_type x9, other arithmetic, low(): return x.astype(jnp.bfloat16)  17.9 us
    ppermute x3, waiting for transfers between devices, shards(): lax.ppermute(came['L', s], 'seq', [(i, i + 1) for i in range(s, seq - 1)])  16 us
    ppermute x15, starting transfers between devices, partner(): return (x, lambda x: lax.ppermute(x, axis, paths))  13.7 us
  transfers between devices with their start and end apart: 28, of which 17 were waited for; matrix products, arithmetic and copies ran while one was open for 26% of the time, Pallas kernels for 16%

profile of v2, /device:TPU:26, one launch (start us, length us, event | category | flops | bytes accessed | tf_op | source)
XLA Modules:
  0.0 395.2 jit_solution(709313843720125313)
XLA Ops:
  19.7 7.3 %attend_forward.4 = (f32[768,512]{1,0:T(8,128)S(1)}, f32[6,2,512]{2,1,0:T(2,128)S(1)}, f32[6,2,512]{2,1,0:T(2,128)S(1)}) custom-call(bf16[512,768]{1,0:T(8,128)(2,1)S(1)} %fusion.28.q_ref, bf16[512,1536]{1,0:T(8,128)(2,1)} %fusion.26.k_ref.v_ref, bf16[512,1536]{1,0:T(8,128)(2,1)} %fusion.26.k_ref.v_ref, s32[1,512]{1,0:T(1,128)S(1)} %copy-done.48, ...), custom_call_target="tpu_custom_call" | custom-call | flops 512 | bytes 512 | tf_op jit(solution)/shard_map/attend_forward/pallas_call | solution.py:145
  28.8 5.1 %collective-permute-done.15 = bf16[520,768]{1,0:T(8,128)(2,1)} collective-permute-done((bf16[520,768]{1,0:T(8,128)(2,1)S(1)}, bf16[520,768]{1,0:T(8,128)(2,1)}, u32[]{:S(2)}, u32[]{:S(2)}) %collective-permute-start.15) | collective-permute-done | bytes 798752 | tf_op jit(solution)/shard_map/ppermute | solution.py:425
  42.3 6.6 %attend_forward.5 = (f32[768,512]{1,0:T(8,128)S(1)}, f32[6,2,512]{2,1,0:T(2,128)S(1)}, f32[6,2,512]{2,1,0:T(2,128)S(1)}) custom-call(bf16[512,768]{1,0:T(8,128)(2,1)S(1)} %copy-done.9, bf16[512,1536]{1,0:T(8,128)(2,1)S(1)} %fusion.22.k_ref.v_ref, bf16[512,1536]{1,0:T(8,128)(2,1)S(1)} %fusion.22.k_ref.v_ref, s32[1,512]{1,0:T(1,128)S(1)} %copy-done.48, ...), custom_call_target="tpu_custom_call" | custom-call | flops 512 | bytes 512 | tf_op jit(solution)/shard_map/attend_forward/pallas_call | solution.py:145
  48.9 5.6 %collective-permute-done.17 = bf16[520,768]{1,0:T(8,128)(2,1)} collective-permute-done((bf16[520,768]{1,0:T(8,128)(2,1)}, bf16[520,768]{1,0:T(8,128)(2,1)}, u32[]{:S(2)}, u32[]{:S(2)}) %collective-permute-start.17) | collective-permute-done | bytes 798752 | tf_op jit(solution)/shard_map/ppermute | solution.py:425
  62.2 6.6 %attend_forward.6 = (f32[768,512]{1,0:T(8,128)S(1)}, f32[6,2,512]{2,1,0:T(2,128)S(1)}, f32[6,2,512]{2,1,0:T(2,128)S(1)}) custom-call(bf16[512,768]{1,0:T(8,128)(2,1)S(1)} %copy-done.10, bf16[512,1536]{1,0:T(8,128)(2,1)S(1)} %fusion.23.k_ref.v_ref, bf16[512,1536]{1,0:T(8,128)(2,1)S(1)} %fusion.23.k_ref.v_ref, s32[1,512]{1,0:T(1,128)S(1)} %copy-done.48, ...), custom_call_target="tpu_custom_call" | custom-call | flops 512 | bytes 512 | tf_op jit(solution)/shard_map/attend_forward/pallas_call | solution.py:145
  68.8 5.3 %collective-permute-done.19 = bf16[520,768]{1,0:T(8,128)(2,1)} collective-permute-done((bf16[520,768]{1,0:T(8,128)(2,1)}, bf16[520,768]{1,0:T(8,128)(2,1)}, u32[]{:S(2)}, u32[]{:S(2)}) %collective-permute-start.19) | collective-permute-done | bytes 798752 | tf_op jit(solution)/shard_map/ppermute | solution.py:425
  78.8 8.9 %attend_forward.7 = (f32[768,512]{1,0:T(8,128)}, f32[6,2,512]{2,1,0:T(2,128)S(1)}, bf16[512,768]{1,0:T(8,128)(2,1)S(1)}) custom-call(bf16[512,768]{1,0:T(8,128)(2,1)S(1)} %copy-done.11, bf16[512,1536]{1,0:T(8,128)(2,1)} %fusion.24.k_ref.v_ref, bf16[512,1536]{1,0:T(8,128)(2,1)} %fusion.24.k_ref.v_ref, s32[1,512]{1,0:T(1,128)S(1)} %copy-done.48, ...), custom_call_target="tpu_custom_call" | custom-call | flops 512 | bytes 512 | tf_op jit(solution)/shard_map/attend_forward/pallas_call | solution.py:145
  91.2 5.6 %fusion.21 = (bf16[512,3072]{1,0:T(8,128)(2,1)S(1)}, bf16[512,3072]{1,0:T(8,128)(2,1)S(1)}) fusion(f32[3072]{0:T(1024)S(1)} %copy-done.63, bf16[768,3072]{1,0:T(8,128)(2,1)S(1)} %bitcast.78, f32[512,768]{1,0:T(8,128)S(1)} %subtract_multiply_fusion.3, f32[768]{0:T(1024)S(1)} %copy-done.67, f32[768]{0:T(1024)S(1)} %copy-done.52), kind=kOutput, calls=%fused_computation.66 | convolution fusion | flops 2435973120 | bytes 12601344 | tf_op jit(solution)/shard_map/dot_general | solution.py:25
  103.3 4.7 %convolution_convert_fusion.8 = bf16[3072,768]{1,0:T(8,128)(2,1)} fusion(bf16[512,3072]{1,0:T(8,128)(2,1)S(1)} %get-tuple-element.294, f32[512,768]{1,0:T(8,128)S(1)} %get-tuple-element.416), kind=kOutput, calls=%fused_computation.71 | convolution fusion | flops 2418671616 | bytes 9437184 | tf_op jit(solution)/shard_map/dot_general | solution.py:25
  119.3 92.8 %conditional.6 = (bf16[384,3072]{0,1:T(8,128)(2,1)}, f32[12,768]{1,0:T(8,128)}, f32[512,768]{1,0:T(8,128)}, bf16[512,768]{1,0:T(8,128)(2,1)}, bf16[512,768]{1,0:T(8,128)(2,1)}, /*index=5*/bf16[512,768]{1,0:T(8,128)(2,1)}) conditional(s32[]{:T(128)} %bitcast.10, () %tuple.78, (f32[512]{0:T(512)S(1)}, bf16[512,3072]{1,0:T(8,128)(2,1)}, ...), branch_computations={%region_6.7_spmd, %region_7.17_spmd} | conditional | flops 14535235584 | bytes 290072832 | solution.py:350
  119.4 8.5 %multiply_reduce_fusion.1 = (f32[768]{0:T(1024)S(1)}, f32[512]{0:T(512)S(1)}, f32[512]{0:T(512)S(1)}, f32[768]{0:T(1024)S(1)}, f32[512,768]{1,0:T(8,128)}) fusion(f32[512,768]{1,0:T(8,128)} %get-tuple-element.129, f32[768]{0:T(1024)S(1)} %get-tuple-element.128, f32[512,768]{1,0:T(8,128)} %get-tuple-element.125, bf16[512,3072]{1,0:T(8,128)(2,1)} %get-tuple-element.126, ...), kind=kOutput, calls=%fused_computation.7 | convolution fusion | flops 2419062272 | bytes 12596224 | tf_op jit(solution)/shard_map/cond/branch_1_fun/dot_general | solution.py:25
  134.7 11.6 %attend_backward.4 = (bf16[512,1536]{1,0:T(8,128)(2,1)S(1)}, f32[2,768]{1,0:T(2,128)S(1)}, f32[768,512]{1,0:T(8,128)S(1)}) custom-call(bf16[512,768]{1,0:T(8,128)(2,1)} %copy-done.12, bf16[512,768]{1,0:T(8,128)(2,1)S(1)} %convolution_convert_fusion.2.g_ref, bf16[512,1536]{1,0:T(8,128)(2,1)} %get-tuple-element.140.k_ref.v_ref, ...), custom_call_target="tpu_custom_call" | custom-call | flops 512 | bytes 512 | tf_op jit(solution)/shard_map/cond/branch_1_fun/attend_backward/pallas_call | solution.py:248
  146.3 10.6 %attend_backward.5 = (bf16[512,1536]{1,0:T(8,128)(2,1)S(1)}, f32[2,768]{1,0:T(2,128)S(1)}, f32[768,512]{1,0:T(8,128)S(1)}) custom-call(bf16[512,768]{1,0:T(8,128)(2,1)S(1)} %copy-done.13, bf16[512,768]{1,0:T(8,128)(2,1)S(1)} %convolution_convert_fusion.2.g_ref, bf16[512,1536]{1,0:T(8,128)(2,1)S(1)} %copy-done.18, bf16[512,1536]{1,0:T(8,128)(2,1)S(1)} %copy-done.18, ...), custom_call_target="tpu_custom_call" | custom-call | flops 512 | bytes 512 | tf_op jit(solution)/shard_map/cond/branch_1_fun/attend_backward/pallas_call | solution.py:248
  157.0 10.6 %attend_backward.6 = (bf16[512,1536]{1,0:T(8,128)(2,1)S(1)}, f32[2,768]{1,0:T(2,128)S(1)}, f32[768,512]{1,0:T(8,128)S(1)}) custom-call(bf16[512,768]{1,0:T(8,128)(2,1)S(1)} %copy-done.13, bf16[512,768]{1,0:T(8,128)(2,1)S(1)} %convolution_convert_fusion.2.g_ref, bf16[512,1536]{1,0:T(8,128)(2,1)S(1)} %copy-done.16, bf16[512,1536]{1,0:T(8,128)(2,1)S(1)} %copy-done.16, ...), custom_call_target="tpu_custom_call" | custom-call | flops 512 | bytes 512 | tf_op jit(solution)/shard_map/cond/branch_1_fun/attend_backward/pallas_call | solution.py:248
  167.6 11.7 %attend_backward.7 = (bf16[512,1536]{1,0:T(8,128)(2,1)S(1)}, f32[2,768]{1,0:T(2,128)S(1)}, bf16[512,768]{1,0:T(8,128)(2,1)S(1)}) custom-call(bf16[512,768]{1,0:T(8,128)(2,1)S(1)} %copy-done.13, bf16[512,768]{1,0:T(8,128)(2,1)S(1)} %convolution_convert_fusion.2.g_ref, bf16[512,1536]{1,0:T(8,128)(2,1)S(1)} %copy-done.14, bf16[512,1536]{1,0:T(8,128)(2,1)S(1)} %copy-done.14, ...), custom_call_target="tpu_custom_call" | custom-call | flops 512 | bytes 512 | tf_op jit(solution)/shard_map/cond/branch_1_fun/attend_backward/pallas_call | solution.py:248
  216.0 41.5 %conditional.7 = (bf16[96,3072]{1,0:T(8,128)(2,1)}, f32[12,768]{1,0:T(8,128)}, f32[512,768]{1,0:T(8,128)}, f32[512,768]{1,0:T(8,128)}, f32[512,768]{1,0:T(8,128)}, /*index=5*/f32[512,768]{1,0:T(8,128)}) conditional(s32[]{:T(128)} %bitcast.10, () %tuple.83, (bf16[384,3072]{0,1:T(8,128)(2,1)}, f32[12,768]{1,0:T(8,128)}, s32[]{:T(128)}, ...), branch_computations={%region_17.18_spmd, %region_18.19_spmd} | conditional | flops 7489614 | bytes 29811720 | solution.py:350
  219.4 17.4 %collective-permute-done = bf16[192,3072]{1,0:T(8,128)(2,1)} collective-permute-done((bf16[192,3072]{1,0:T(8,128)(2,1)S(1)}, bf16[192,3072]{1,0:T(8,128)(2,1)}, u32[]{:S(2)}, u32[]{:S(2)}) %collective-permute-start) | collective-permute-done | bytes 1179680 | tf_op jit(solution)/shard_map/cond/branch_1_fun/ppermute | solution.py:313
  240.7 5.0 %collective-permute-done.2 = f32[12,768]{1,0:T(8,128)S(1)} collective-permute-done((f32[12,768]{1,0:T(8,128)}, f32[12,768]{1,0:T(8,128)S(1)}, u32[]{:S(2)}, u32[]{:S(2)}) %collective-permute-start.2) | collective-permute-done | bytes 36896 | tf_op jit(solution)/shard_map/cond/branch_1_fun/ppermute | solution.py:313
  257.5 55.0 %conditional.8 = (bf16[96,3072]{1,0:T(8,128)(2,1)S(1)}, f32[12,768]{1,0:T(8,128)}, bf16[1,768]{1,0:T(2,128)(2,1)S(1)}, bf16[1,768]{1,0:T(2,128)(2,1)S(1)}, bf16[...) conditional(s32[]{:T(128)} %bitcast.10, () %tuple.81, ...), branch_computations={%region_19.20_spmd, %region_20.21_spmd} | conditional | flops 4890676 | bytes 8147904 | solution.py:350
  258.6 8.9 %collective-permute-done.6 = bf16[48,3072]{1,0:T(8,128)(2,1)S(1)} collective-permute-done((bf16[48,3072]{1,0:T(8,128)(2,1)S(1)}, bf16[48,3072]{1,0:T(8,128)(2,1)S(1)}, u32[]{:S(2)}, u32[]{:S(2)}) %collective-permute-start.6) | collective-permute-done | bytes 294944 | tf_op jit(solution)/shard_map/cond/branch_1_fun/ppermute | solution.py:313
  270.6 11.3 %collective-permute-done.7 = bf16[24,3072]{1,0:T(8,128)(2,1)S(1)} collective-permute-done((bf16[24,3072]{1,0:T(8,128)(2,1)S(1)}, bf16[24,3072]{1,0:T(8,128)(2,1)S(1)}, u32[]{:S(2)}, u32[]{:S(2)}) %collective-permute-start.7) | collective-permute-done | bytes 147488 | tf_op jit(solution)/shard_map/cond/branch_1_fun/ppermute | solution.py:313
  283.4 9.9 %collective-permute-done.8 = bf16[24,3072]{1,0:T(8,128)(2,1)S(1)} collective-permute-done((bf16[24,3072]{1,0:T(8,128)(2,1)S(1)}, bf16[24,3072]{1,0:T(8,128)(2,1)S(1)}, u32[]{:S(2)}, u32[]{:S(2)}) %collective-permute-start.8) | collective-permute-done | bytes 147488 | tf_op jit(solution)/shard_map/cond/branch_1_fun/ppermute | solution.py:313
  296.3 12.3 %collective-permute-done.11 = f32[12,768]{1,0:T(8,128)S(1)} collective-permute-done((f32[12,768]{1,0:T(8,128)S(1)}, f32[12,768]{1,0:T(8,128)S(1)}, u32[]{:S(2)}, u32[]{:S(2)}) %collective-permute-start.11) | collective-permute-done | bytes 36896 | tf_op jit(solution)/shard_map/cond/branch_1_fun/ppermute | solution.py:313
  318.1 5.0 %collective-permute-start.23 = (bf16[512,768]{1,0:T(8,128)(2,1)}, bf16[512,768]{1,0:T(8,128)(2,1)}, u32[]{:S(2)}, u32[]{:S(2)}) collective-permute-start(bf16[512,768]{1,0:T(8,128)(2,1)} %add_convert_fusion.10), channel_id=1, source_target_pairs={{2,1},{3,2},{6,5},{7,6},{10,9},{11,10},{14,13},{15,14},{18,17},{19... | collective-permute-start | bytes 2359304 | tf_op jit(solution)/shard_map/ppermute | solution.py:517
  324.7 10.8 %conditional.9 = (bf16[192,3072]{1,0:T(8,128)(2,1)S(1)}) conditional(s32[]{:T(128)} %bitcast.10, () %tuple.89, bf16[96,3072]{1,0:T(8,128)(2,1)S(1)} %get-tuple-element.319), branch_computations={%region_21.22_spmd, %region_22.23_spmd} | conditional | flops 5308473 | bytes 4719212 | solution.py:350
  327.4 7.9 %collective-permute-done.4 = bf16[96,3072]{1,0:T(8,128)(2,1)S(1)} collective-permute-done((bf16[96,3072]{1,0:T(8,128)(2,1)S(1)}, bf16[96,3072]{1,0:T(8,128)(2,1)S(1)}, u32[]{:S(2)}, u32[]{:S(2)}) %collective-permute-start.4) | collective-permute-done | bytes 589856 | tf_op jit(solution)/shard_map/cond/branch_1_fun/ppermute | solution.py:313
  335.7 18.8 %conditional.10 = (bf16[384,3072]{1,0:T(8,128)(2,1)S(1)}, f32[3072,768]{1,0:T(8,128)}, f32[768,3072]{1,0:T(8,128)}) conditional(s32[]{:T(128)} %bitcast.10, () %tuple.88, (bf16[192,3072]{1,0:T(8,128)(2,1)S(1)}, bf16[3072,768]{1,0:T(8,128)(2,1)}, bf16[768,3072]{1,0:T(8,128)(2,1)}) %tuple.90), branch_computations={%region_25.26_spmd, %region_26.27_spmd} | conditional | flops 15335481 | bytes 56623768 | solution.py:350
  338.1 7.0 %convert_element_type.198 = f32[3072,768]{1,0:T(8,128)} convert(bf16[3072,768]{1,0:T(8,128)(2,1)} %get-tuple-element.173) | non-fusion elementwise | flops 2359296 | bytes 14155776 | tf_op jit(solution)/shard_map/cond/branch_1_fun/convert_element_type | solution.py:33
  345.1 5.0 %convert_element_type.199 = f32[768,3072]{1,0:T(8,128)} convert(bf16[768,3072]{1,0:T(8,128)(2,1)S(1)} %copy-done.26) | non-fusion elementwise | flops 2359296 | bytes 14155776 | tf_op jit(solution)/shard_map/cond/branch_1_fun/convert_element_type | solution.py:33
  358.9 5.8 %collective-permute-start.25 = (bf16[512,768]{1,0:T(8,128)(2,1)}, bf16[512,768]{1,0:T(8,128)(2,1)}, u32[]{:S(2)}, u32[]{:S(2)}) collective-permute-start(bf16[512,768]{1,0:T(8,128)(2,1)} %add_convert_fusion.8), channel_id=1, source_target_pairs={{1,0},{2,1},{3,2},{5,4},{6,5},{7,6},{9,8},{10,9},{11,10},{13,12},{... | collective-permute-start | bytes 2359304 | tf_op jit(solution)/shard_map/ppermute | solution.py:517
  366.0 11.8 %conditional.11 = (f32[768,768]{1,0:T(8,128)}, f32[768,768]{1,0:T(8,128)}, f32[768,768]{1,0:T(8,128)}, f32[768,768]{1,0:T(8,128)}) conditional(s32[]{:T(128)} %bitcast.10, () %tuple.93, bf16[384,3072]{1,0:T(8,128)(2,1)S(1)} %get-tuple-element.330), branch_computations={%region_27.28_spmd, %region_28.29_spmd} | conditional | flops 23592976 | bytes 33030360 | solution.py:350
  380.1 4.8 %collective-permute-done.26 = bf16[512,768]{1,0:T(8,128)(2,1)} collective-permute-done((bf16[512,768]{1,0:T(8,128)(2,1)S(1)}, bf16[512,768]{1,0:T(8,128)(2,1)}, u32[]{:S(2)}, u32[]{:S(2)}) %collective-permute-start.26) | collective-permute-done | bytes 786464 | tf_op jit(solution)/shard_map/ppermute | solution.py:518
  (300 shorter events, 169.1 us)
Async XLA Ops:
  7.2 328.5 %all-reduce.5.cloned.1.call-start = ((), (), s32[]{:S(2)}) async-start(), calls=%async_computation | async-start | bytes 18874368 | tf_op jit(solution)/shard_map/psum | solution.py:459
  9.3 19.5 %collective-permute-start.16 = (bf16[520,768]{1,0:T(8,128)(2,1)S(1)}, bf16[520,768]{1,0:T(8,128)(2,1)}, u32[]{:S(2)}, u32[]{:S(2)}) collective-permute-start(bf16[520,768]{1,0:T(8,128)(2,1)S(1)} %pad_maximum_fusion.1), channel_id=1, source_target_pairs={{1,0},{2,1},{3,2},{5,4},{6,5},{7,6},{9,8},{10,9},{11,10},{13,12},{... | collective-permute-start | bytes 2396168 | tf_op jit(solution)/shard_map/ppermute | solution.py:426
  12.7 21.3 %collective-permute-start.15 = (bf16[520,768]{1,0:T(8,128)(2,1)S(1)}, bf16[520,768]{1,0:T(8,128)(2,1)}, u32[]{:S(2)}, u32[]{:S(2)}) collective-permute-start(bf16[520,768]{1,0:T(8,128)(2,1)S(1)} %pad_maximum_fusion.1), channel_id=1, source_target_pairs={{0,1},{1,2},{2,3},{4,5},{5,6},{6,7},{8,9},{9,10},{10,11},{12,13},{... | collective-permute-start | bytes 2396168 | tf_op jit(solution)/shard_map/ppermute | solution.py:425
  33.9 20.6 %collective-permute-start.17 = (bf16[520,768]{1,0:T(8,128)(2,1)}, bf16[520,768]{1,0:T(8,128)(2,1)}, u32[]{:S(2)}, u32[]{:S(2)}) collective-permute-start(bf16[520,768]{1,0:T(8,128)(2,1)} %collective-permute-done.15), channel_id=1, source_target_pairs={{1,2},{2,3},{5,6},{6,7},{9,10},{10,11},{13,14},{14,15},{17,18},{18... | collective-permute-start | bytes 2396168 | tf_op jit(solution)/shard_map/ppermute | solution.py:425
  35.2 19.3 %collective-permute-start.18 = (bf16[520,768]{1,0:T(8,128)(2,1)}, bf16[520,768]{1,0:T(8,128)(2,1)}, u32[]{:S(2)}, u32[]{:S(2)}) collective-permute-start(bf16[520,768]{1,0:T(8,128)(2,1)} %collective-permute-done.16), channel_id=1, source_target_pairs={{1,0},{2,1},{5,4},{6,5},{9,8},{10,9},{13,12},{14,13},{17,16},{18,1... | collective-permute-start | bytes 2396168 | tf_op jit(solution)/shard_map/ppermute | solution.py:426
  54.5 19.6 %collective-permute-start.19 = (bf16[520,768]{1,0:T(8,128)(2,1)}, bf16[520,768]{1,0:T(8,128)(2,1)}, u32[]{:S(2)}, u32[]{:S(2)}) collective-permute-start(bf16[520,768]{1,0:T(8,128)(2,1)} %collective-permute-done.17), channel_id=1, source_target_pairs={{2,3},{6,7},{10,11},{14,15},{18,19},{22,23},{26,27},{30,31}} | collective-permute-start | bytes 2396168 | tf_op jit(solution)/shard_map/ppermute | solution.py:425
  57.1 17.0 %collective-permute-start.20 = (bf16[520,768]{1,0:T(8,128)(2,1)}, bf16[520,768]{1,0:T(8,128)(2,1)}, u32[]{:S(2)}, u32[]{:S(2)}) collective-permute-start(bf16[520,768]{1,0:T(8,128)(2,1)} %collective-permute-done.18), channel_id=1, source_target_pairs={{1,0},{5,4},{9,8},{13,12},{17,16},{21,20},{25,24},{29,28}} | collective-permute-start | bytes 2396168 | tf_op jit(solution)/shard_map/ppermute | solution.py:426
  78.8 12.0 %slice-start.2 = ((s8[4718592]{0:T(1024)(128)(4,1)}), s8[4194304]{0:T(1024)(128)(4,1)S(1)}, s32[]{:S(2)}) async-start(s8[4718592]{0:T(1024)(128)(4,1)} %bitcast.77), calls=%async_computation.3 | async-start | bytes 8388608
  91.2 19.8 %copy-start.24 = (f32[512,768]{1,0:T(8,128)}, f32[512,768]{1,0:T(8,128)S(1)}, u32[]{:S(2)}) copy-start(f32[512,768]{1,0:T(8,128)S(1)} %subtract_multiply_fusion.3) | copy-start | bytes 4718596
  156.9 25.6 %copy-start = (bf16[512,1536]{1,0:T(8,128)(2,1)}, bf16[512,1536]{1,0:T(8,128)(2,1)S(1)}, u32[]{:S(2)}) copy-start(bf16[512,1536]{1,0:T(8,128)(2,1)S(1)} %get-tuple-element.149) | copy-start | bytes 4718596 | tf_op jit(solution)/shard_map/cond
  167.6 16.5 %copy-start.2 = (bf16[512,1536]{1,0:T(8,128)(2,1)}, bf16[512,1536]{1,0:T(8,128)(2,1)S(1)}, u32[]{:S(2)}) copy-start(bf16[512,1536]{1,0:T(8,128)(2,1)S(1)} %get-tuple-element.151) | copy-start | bytes 4718596 | tf_op jit(solution)/shard_map/cond
  191.1 16.4 %collective-permute-start.13 = (bf16[384,3072]{0,1:T(8,128)(2,1)}, bf16[384,3072]{0,1:T(8,128)(2,1)}, u32[]{:S(2)}, u32[]{:S(2)}) collective-permute-start(bf16[384,3072]{0,1:T(8,128)(2,1)} %constant_dynamic-slice_fusion), channel_id=1, source_target_pairs={{0,4},{4,0},{8,12},{12,8},{16,20},{20,16},{24,28},{28,24},{1,5},{5... | collective-permute-start | bytes 7077896 | tf_op jit(solution)/shard_map/cond/branch_1_fun/ppermute | solution.py:313
  194.5 12.4 %collective-permute-start.14 = (f32[12,768]{1,0:T(8,128)S(1)}, f32[12,768]{1,0:T(8,128)S(1)}, u32[]{:S(2)}, u32[]{:S(2)}) collective-permute-start(f32[12,768]{1,0:T(8,128)S(1)} %stack.38), channel_id=1, source_target_pairs={{0,4},{4,0},{8,12},{12,8},{16,20},{20,16},{24,28},{28,24},{1,5},{5... | collective-permute-start | bytes 110600 | tf_op jit(solution)/shard_map/cond/branch_1_fun/ppermute | solution.py:313
  212.2 45.3 %collective-permute-start.21 = (bf16[512,768]{1,0:T(8,128)(2,1)}, bf16[512,768]{1,0:T(8,128)(2,1)}, u32[]{:S(2)}, u32[]{:S(2)}) collective-permute-start(bf16[512,768]{1,0:T(8,128)(2,1)} %get-tuple-element.303), channel_id=1, source_target_pairs={{3,2},{7,6},{11,10},{15,14},{19,18},{23,22},{27,26},{31,30}} | collective-permute-start | bytes 2359304 | tf_op jit(solution)/shard_map/ppermute | solution.py:517
  214.4 43.1 %collective-permute-start.22 = (bf16[512,768]{1,0:T(8,128)(2,1)}, bf16[512,768]{1,0:T(8,128)(2,1)}, u32[]{:S(2)}, u32[]{:S(2)}) collective-permute-start(bf16[512,768]{1,0:T(8,128)(2,1)} %get-tuple-element.303), channel_id=1, source_target_pairs={{0,1},{4,5},{8,9},{12,13},{16,17},{20,21},{24,25},{28,29}} | collective-permute-start | bytes 2359304 | tf_op jit(solution)/shard_map/ppermute | solution.py:518
  218.9 18.0 %collective-permute-start = (bf16[192,3072]{1,0:T(8,128)(2,1)S(1)}, bf16[192,3072]{1,0:T(8,128)(2,1)}, u32[]{:S(2)}, u32[]{:S(2)}) collective-permute-start(bf16[192,3072]{1,0:T(8,128)(2,1)S(1)} %constant_dynamic-slice_fusion.2), channel_id=1, source_target_pairs={{0,8},{4,20},{8,0},{12,28},{16,24},{20,4},{24,16},{28,12},{1,9},{5... | collective-permute-start | bytes 3538952 | tf_op jit(solution)/shard_map/cond/branch_1_fun/ppermute | solution.py:313
  238.6 17.9 %collective-permute-start.1 = (bf16[96,3072]{1,0:T(8,128)(2,1)S(1)}, bf16[96,3072]{1,0:T(8,128)(2,1)S(1)}, u32[]{:S(2)}, u32[]{:S(2)}) collective-permute-start(bf16[96,3072]{1,0:T(8,128)(2,1)S(1)} %constant_dynamic-slice_fusion.1), channel_id=1, source_target_pairs={{0,16},{4,12},{8,24},{12,4},{16,0},{20,28},{24,8},{28,20},{1,17},{... | collective-permute-start | bytes 1769480 | tf_op jit(solution)/shard_map/cond/branch_1_fun/ppermute | solution.py:313
  240.2 5.5 %collective-permute-start.2 = (f32[12,768]{1,0:T(8,128)}, f32[12,768]{1,0:T(8,128)S(1)}, u32[]{:S(2)}, u32[]{:S(2)}) collective-permute-start(f32[12,768]{1,0:T(8,128)} %get-tuple-element.165), channel_id=1, source_target_pairs={{0,8},{4,20},{8,0},{12,28},{16,24},{20,4},{24,16},{28,12},{1,9},{5... | collective-permute-start | bytes 110600 | tf_op jit(solution)/shard_map/cond/branch_1_fun/ppermute | solution.py:313
  246.5 9.4 %collective-permute-start.3 = (f32[12,768]{1,0:T(8,128)S(1)}, f32[12,768]{1,0:T(8,128)S(1)}, u32[]{:S(2)}, u32[]{:S(2)}) collective-permute-start(f32[12,768]{1,0:T(8,128)S(1)} %add.276), channel_id=1, source_target_pairs={{0,16},{4,12},{8,24},{12,4},{16,0},{20,28},{24,8},{28,20},{1,17},{... | collective-permute-start | bytes 110600 | tf_op jit(solution)/shard_map/cond/branch_1_fun/ppermute | solution.py:313
  258.5 9.1 %collective-permute-start.6 = (bf16[48,3072]{1,0:T(8,128)(2,1)S(1)}, bf16[48,3072]{1,0:T(8,128)(2,1)S(1)}, u32[]{:S(2)}, u32[]{:S(2)}) collective-permute-start(bf16[48,3072]{1,0:T(8,128)(2,1)S(1)} %constant_dynamic-slice_fusion.4), channel_id=1, source_target_pairs={{0,1},{1,0},{2,3},{3,2},{4,5},{5,4},{6,7},{7,6},{8,9},{9,8},{10,11... | collective-permute-start | bytes 884744 | tf_op jit(solution)/shard_map/cond/branch_1_fun/ppermute | solution.py:313
  268.7 13.2 %collective-permute-start.7 = (bf16[24,3072]{1,0:T(8,128)(2,1)S(1)}, bf16[24,3072]{1,0:T(8,128)(2,1)S(1)}, u32[]{:S(2)}, u32[]{:S(2)}) collective-permute-start(bf16[24,3072]{1,0:T(8,128)(2,1)S(1)} %constant_dynamic-slice_fusion.3), channel_id=1, source_target_pairs={{0,2},{1,3},{2,0},{3,1},{4,6},{5,7},{6,4},{7,5},{8,10},{9,11},{10,... | collective-permute-start | bytes 442376 | tf_op jit(solution)/shard_map/cond/branch_1_fun/ppermute | solution.py:313
  282.0 11.4 %collective-permute-start.8 = (bf16[24,3072]{1,0:T(8,128)(2,1)S(1)}, bf16[24,3072]{1,0:T(8,128)(2,1)S(1)}, u32[]{:S(2)}, u32[]{:S(2)}) collective-permute-start(bf16[24,3072]{1,0:T(8,128)(2,1)S(1)} %add_convert_fusion.5), channel_id=1, source_target_pairs={{0,2},{1,3},{2,0},{3,1},{4,6},{5,7},{6,4},{7,5},{8,10},{9,11},{10,... | collective-permute-start | bytes 442376 | tf_op jit(solution)/shard_map/cond/branch_1_fun/ppermute | solution.py:313
  282.0 11.5 %collective-permute-start.10 = (f32[12,768]{1,0:T(8,128)}, f32[12,768]{1,0:T(8,128)S(1)}, u32[]{:S(2)}, u32[]{:S(2)}) collective-permute-start(f32[12,768]{1,0:T(8,128)} %get-tuple-element.171), channel_id=1, source_target_pairs={{0,1},{1,0},{2,3},{3,2},{4,5},{5,4},{6,7},{7,6},{8,9},{9,8},{10,11... | collective-permute-start | bytes 110600 | tf_op jit(solution)/shard_map/cond/branch_1_fun/ppermute | solution.py:313
  293.4 19.0 %collective-permute-start.9 = (bf16[48,3072]{1,0:T(8,128)(2,1)S(1)}, bf16[48,3072]{1,0:T(8,128)(2,1)S(1)}, u32[]{:S(2)}, u32[]{:S(2)}) collective-permute-start(bf16[48,3072]{1,0:T(8,128)(2,1)S(1)} %maximum_select_fusion.7), channel_id=1, source_target_pairs={{0,1},{1,0},{2,3},{3,2},{4,5},{5,4},{6,7},{7,6},{8,9},{9,8},{10,11... | collective-permute-start | bytes 884744 | tf_op jit(solution)/shard_map/cond/branch_1_fun/ppermute | solution.py:313
  294.3 14.3 %collective-permute-start.11 = (f32[12,768]{1,0:T(8,128)S(1)}, f32[12,768]{1,0:T(8,128)S(1)}, u32[]{:S(2)}, u32[]{:S(2)}) collective-permute-start(f32[12,768]{1,0:T(8,128)S(1)} %add.286), channel_id=1, source_target_pairs={{0,2},{1,3},{2,0},{3,1},{4,6},{5,7},{6,4},{7,5},{8,10},{9,11},{10,... | collective-permute-start | bytes 110600 | tf_op jit(solution)/shard_map/cond/branch_1_fun/ppermute | solution.py:313
  318.1 36.4 %collective-permute-start.23 = (bf16[512,768]{1,0:T(8,128)(2,1)}, bf16[512,768]{1,0:T(8,128)(2,1)}, u32[]{:S(2)}, u32[]{:S(2)}) collective-permute-start(bf16[512,768]{1,0:T(8,128)(2,1)} %add_convert_fusion.10), channel_id=1, source_target_pairs={{2,1},{3,2},{6,5},{7,6},{10,9},{11,10},{14,13},{15,14},{18,17},{19... | collective-permute-start | bytes 2359304 | tf_op jit(solution)/shard_map/ppermute | solution.py:517
  323.1 31.4 %collective-permute-start.24 = (bf16[512,768]{1,0:T(8,128)(2,1)}, bf16[512,768]{1,0:T(8,128)(2,1)}, u32[]{:S(2)}, u32[]{:S(2)}) collective-permute-start(bf16[512,768]{1,0:T(8,128)(2,1)} %add_convert_fusion.9), channel_id=1, source_target_pairs={{0,1},{1,2},{4,5},{5,6},{8,9},{9,10},{12,13},{13,14},{16,17},{17,1... | collective-permute-start | bytes 2359304 | tf_op jit(solution)/shard_map/ppermute | solution.py:518
  324.7 10.6 %collective-permute-start.4 = (bf16[96,3072]{1,0:T(8,128)(2,1)S(1)}, bf16[96,3072]{1,0:T(8,128)(2,1)S(1)}, u32[]{:S(2)}, u32[]{:S(2)}) collective-permute-start(bf16[96,3072]{1,0:T(8,128)(2,1)S(1)} %param.7), channel_id=1, source_target_pairs={{0,16},{4,12},{8,24},{12,4},{16,0},{20,28},{24,8},{28,20},{1,17},{... | collective-permute-start | bytes 1769480 | tf_op jit(solution)/shard_map/cond/branch_1_fun/ppermute | solution.py:313
  335.7 16.7 %collective-permute-start.5 = (bf16[192,3072]{1,0:T(8,128)(2,1)S(1)}, bf16[192,3072]{1,0:T(8,128)(2,1)}, u32[]{:S(2)}, u32[]{:S(2)}) collective-permute-start(bf16[192,3072]{1,0:T(8,128)(2,1)S(1)} %get-tuple-element.172), channel_id=1, source_target_pairs={{0,8},{4,20},{8,0},{12,28},{16,24},{20,4},{24,16},{28,12},{1,9},{5... | collective-permute-start | bytes 3538952 | tf_op jit(solution)/shard_map/cond/branch_1_fun/ppermute | solution.py:313
  358.9 21.2 %collective-permute-start.25 = (bf16[512,768]{1,0:T(8,128)(2,1)}, bf16[512,768]{1,0:T(8,128)(2,1)}, u32[]{:S(2)}, u32[]{:S(2)}) collective-permute-start(bf16[512,768]{1,0:T(8,128)(2,1)} %add_convert_fusion.8), channel_id=1, source_target_pairs={{1,0},{2,1},{3,2},{5,4},{6,5},{7,6},{9,8},{10,9},{11,10},{13,12},{... | collective-permute-start | bytes 2359304 | tf_op jit(solution)/shard_map/ppermute | solution.py:517
  364.7 20.2 %collective-permute-start.26 = (bf16[512,768]{1,0:T(8,128)(2,1)S(1)}, bf16[512,768]{1,0:T(8,128)(2,1)}, u32[]{:S(2)}, u32[]{:S(2)}) collective-permute-start(bf16[512,768]{1,0:T(8,128)(2,1)S(1)} %add_convert_fusion.7), channel_id=1, source_target_pairs={{0,1},{1,2},{2,3},{4,5},{5,6},{6,7},{8,9},{9,10},{10,11},{12,13},{... | collective-permute-start | bytes 2359304 | tf_op jit(solution)/shard_map/ppermute | solution.py:518
  366.1 4.7 %collective-permute-start.12 = (bf16[384,3072]{1,0:T(8,128)(2,1)S(1)}, bf16[384,3072]{1,0:T(8,128)(2,1)}, u32[]{:S(2)}, u32[]{:S(2)}) collective-permute-start(bf16[384,3072]{1,0:T(8,128)(2,1)S(1)} %param.11), channel_id=1, source_target_pairs={{0,4},{4,0},{8,12},{12,8},{16,20},{20,16},{24,28},{28,24},{1,5},{5... | collective-permute-start | bytes 7077896 | tf_op jit(solution)/shard_map/cond/branch_1_fun/ppermute | solution.py:313
  (68 other events, 264.2 us)
Sparse Core Ops, SparseCore 0:
  117.0 218.6 all-reduce.4

commit v3 on v2

--- a/solution.py
+++ b/solution.py
@@ -335,6 +335,11 @@
     return add_low(pick(x, side, 2), passed(pick(x, 1 - side, 2), step, counts))
 
 
+def parted(x, step):
+    side = side_of(step)
+    return pick(x, side, 2), pick(x, 1 - side, 2)
+
+
 def up(x, step, counts):
     return join(x, passed(x, step, counts), side_of(step))
 
@@ -462,8 +467,10 @@
     steps = steps_of(**counts)
     far = len(steps) - 1
 
+    chips = [i for i, step in enumerate(steps) if i > 0 and step[0] == "batch"]
+    places = [i for i, step in enumerate(steps) if step[0] == "seq"]
+
     def attention_part():
-        grad_inner_bias = column_sums(grad_inner)
         grad_first = grad_mix + times_back(grad_inner, inner_weight)
         grad_resid, grad_first_gain, grad_first_shift = norm_back(
             grad_first, first_scaled, first_inverse, first_gain
@@ -485,22 +492,9 @@
         late = jnp.concatenate(
             [low(weight_grad(hidden, grad_query)), low(kv_grad), low(weight_grad(attended, grad_branch))], axis=1
         )
-        vectors = jnp.stack(
-            [
-                sums[1],
-                grad_value_bias,
-                column_sums(grad_branch),
-                grad_first_gain,
-                grad_first_shift,
-                grad_outer_bias,
-                grad_second_gain,
-                grad_second_shift,
-                *jnp.split(grad_inner_bias, inner_weight.shape[1] // width),
-            ]
-        )
+        vectors = [sums[1], grad_value_bias, column_sums(grad_branch), grad_first_gain, grad_first_shift]
         own_terms = grad_resid + high(terms[0]) + times_back(grad_query, query_weight)
-        vectors = vectors + passed(vectors, steps[0], counts)
-        return down(late, steps[0], counts), vectors, own_terms, [terms[s] for s in range(1, seq)]
+        return parted(down(late, steps[0], counts), steps[chips[0]]), vectors, own_terms, [terms[s] for s in range(1, seq)]
 
     late, sums, own_terms, terms = apart(certain, attention_part)
     terms = dict(enumerate(terms, 1))
@@ -518,46 +512,57 @@
             lax.ppermute(sends[1], "seq", [(i, i + 1) for i in range(seq - s)]),
         ]
 
-    chips = [i for i, step in enumerate(steps) if i > 0 and step[0] == "batch"]
-    places = [i for i, step in enumerate(steps) if step[0] == "seq"]
-
-    def down_chips(late, sums):
+
+    def down_chips(late, vectors):
+        sums = jnp.stack(
+            [
+                *vectors,
+                grad_outer_bias,
+                grad_second_gain,
+                grad_second_shift,
+                *jnp.split(column_sums(grad_inner), inner_weight.shape[1] // width),
+            ]
+        )
+        sums = sums + passed(sums, steps[0], counts)
         for i in chips:
             sums = sums + passed(sums, steps[i], counts)
-            late = down(late, steps[i], counts)
+            if i == chips[0]:
+                late = add_low(late[0], passed(late[1], steps[i], counts))
+            else:
+                late = down(late, steps[i], counts)
         return late, sums, {s: homeward(s) for s in range(1, seq - 1)}
 
-    def along_row(late, sums):
+    def along_row(late, sums, on_way):
         for i in places:
             sums = sums + passed(sums, steps[i], counts)
             late = down(late, steps[i], counts)
         for i in places[::-1]:
             late = up(late, steps[i], counts)
-        return late, sums
+        return late, sums, [low(high(x) + high(o)) for x, o in zip(found[seq - 2], on_way)]
 
     late, on_way = lax.optimization_barrier((late, homeward(seq - 1)))
     on_way = send(seq - 1, on_way)
     late, sums, found = apart(certain, functools.partial(down_chips, late, sums))
     on_way, late, sums = lax.optimization_barrier((on_way, late, sums))
-    late, sums = apart(certain, functools.partial(along_row, late, sums))
-    work = [functools.partial(lambda i, x: up(x, steps[i], counts), i) for i in chips[::-1]]
+    late, sums, second = apart(certain, functools.partial(along_row, late, sums, on_way))
+    def up_chips(late):
+        for i in chips[::-1]:
+            late = up(late, steps[i], counts)
+        return late
+
+    def last_part(late, early_sums):
+        return up_last(late, steps[0], counts, (width, 2 * width, 3 * width)), [high(x) for x in early_sums]
+
     for s in reversed(range(1, seq - 1)):
-        totals_home = [low(high(x) + high(o)) for x, o in zip(found[s], on_way)]
+        totals_home = second if s == seq - 2 else [low(high(x) + high(o)) for x, o in zip(found[s], on_way)]
         late, totals_home = lax.optimization_barrier((late, totals_home))
         on_way = send(s, totals_home)
         if s == seq - 2:
-            for i, run in enumerate(work):
-                if i == len(work) - 1:
-                    late, early_sums = apart(
-                        certain, lambda x=late: (run(x), [high(y) for y in early_sums])
-                    )
-                else:
-                    late = apart(certain, functools.partial(run, late))
-                late, early_sums = lax.optimization_barrier((late, early_sums))
+            late = apart(certain, functools.partial(up_chips, late))
             on_way, late = lax.optimization_barrier((on_way, late))
-    late = apart(
-        certain, lambda: up_last(late, steps[0], counts, (width, 2 * width, 3 * width))
-    )
+    late, early_sums = lax.optimization_barrier((late, early_sums))
+    late, early_sums = apart(certain, functools.partial(last_part, late, early_sums))
+    on_way, late, early_sums = lax.optimization_barrier((on_way, late, early_sums))
     vectors = sums
     grad_query_weight, grad_key_weight, grad_value_weight, grad_proj_weight = late
     grad_input = low(own_terms + high(on_way[0]) + high(on_way[1]))

time: 402 us -> 396 us (0.985)
  the two profiles are of different devices: /device:TPU:26 before, /device:TPU:0 now
where the time goes in v3:
time: 396 us; the launch traced here: 389 us
  waiting for transfers between devices  104 us (26%)
  Pallas kernels  74 us (19%)
  matrix products  64.1 us (16%)
  other arithmetic  58.2 us (15%)
  starting transfers between devices  42.7 us (11%)
  local copies, waits for them, and re-layouts  28.8 us (7%)
  between operations  15.7 us (4%)
    ppermute x15, waiting for transfers between devices, partner(): return (x, lambda x: lax.ppermute(x, axis, paths))  82.4 us
    dot_general x24, matrix products, dot(): lax.dot_general(left, right, dims, preferred_element_type=jnp.float32)  64.1 us
    pallas_call x4, Pallas kernels, attend_backward(): pl.pallas_call(functools.partial(backward_kernel, first, last, pairs), gr...  44.5 us
    pallas_call x4, Pallas kernels, attend_forward(): pl.pallas_call(functools.partial(forward_kernel, first, last), grid_spec=...  29.4 us
    convert_element_type x7, other arithmetic, high(): return x.astype(jnp.float32)  24.4 us
    ppermute x3, waiting for transfers between devices, shards(): lax.ppermute(came['R', s], 'seq', [(i, i - 1) for i in range(1, seq - s)])  20.6 us
    convert_element_type x8, other arithmetic, low(): return x.astype(jnp.bfloat16)  15 us
    ppermute x3, starting transfers between devices, send(): lax.ppermute(sends[1], 'seq', [(i, i + 1) for i in range(seq - s)])  12.3 us
  transfers between devices with their start and end apart: 28, of which 15 were waited for; matrix products, arithmetic and copies ran while one was open for 27% of the time, Pallas kernels for 17%

profile of v3, /device:TPU:0, one launch (start us, length us, event | category | flops | bytes accessed | tf_op | source)
XLA Modules:
  0.0 389.0 jit_solution(10334113631963843550)
XLA Ops:
  10.7 6.6 %collective-permute-start.15 = (bf16[520,768]{1,0:T(8,128)(2,1)S(1)}, bf16[520,768]{1,0:T(8,128)(2,1)}, u32[]{:S(2)}, u32[]{:S(2)}) collective-permute-start(bf16[520,768]{1,0:T(8,128)(2,1)S(1)} %pad_maximum_fusion.1), channel_id=1, source_target_pairs={{0,1},{1,2},{2,3},{4,5},{5,6},{6,7},{8,9},{9,10},{10,11},{12,13},{... | collective-permute-start | bytes 2396168 | tf_op jit(solution)/shard_map/ppermute | solution.py:430
  23.0 7.3 %attend_forward.4 = (f32[768,512]{1,0:T(8,128)S(1)}, f32[6,2,512]{2,1,0:T(2,128)S(1)}, f32[6,2,512]{2,1,0:T(2,128)S(1)}) custom-call(bf16[512,768]{1,0:T(8,128)(2,1)S(1)} %fusion.28.q_ref, bf16[512,1536]{1,0:T(8,128)(2,1)} %fusion.26.k_ref.v_ref, bf16[512,1536]{1,0:T(8,128)(2,1)} %fusion.26.k_ref.v_ref, s32[1,512]{1,0:T(1,128)S(1)} %copy-done.50, ...), custom_call_target="tpu_custom_call" | custom-call | flops 512 | bytes 512 | tf_op jit(solution)/shard_map/attend_forward/pallas_call | solution.py:145
  41.7 6.6 %attend_forward.5 = (f32[768,512]{1,0:T(8,128)S(1)}, f32[6,2,512]{2,1,0:T(2,128)S(1)}, f32[6,2,512]{2,1,0:T(2,128)S(1)}) custom-call(bf16[512,768]{1,0:T(8,128)(2,1)S(1)} %copy-done.9, bf16[512,1536]{1,0:T(8,128)(2,1)S(1)} %fusion.22.k_ref.v_ref, bf16[512,1536]{1,0:T(8,128)(2,1)S(1)} %fusion.22.k_ref.v_ref, s32[1,512]{1,0:T(1,128)S(1)} %copy-done.50, ...), custom_call_target="tpu_custom_call" | custom-call | flops 512 | bytes 512 | tf_op jit(solution)/shard_map/attend_forward/pallas_call | solution.py:145
  48.3 10.6 %collective-permute-done.18 = bf16[520,768]{1,0:T(8,128)(2,1)} collective-permute-done((bf16[520,768]{1,0:T(8,128)(2,1)}, bf16[520,768]{1,0:T(8,128)(2,1)}, u32[]{:S(2)}, u32[]{:S(2)}) %collective-permute-start.18) | collective-permute-done | bytes 798752 | tf_op jit(solution)/shard_map/ppermute | solution.py:431
  67.0 6.6 %attend_forward.6 = (f32[768,512]{1,0:T(8,128)S(1)}, f32[6,2,512]{2,1,0:T(2,128)S(1)}, f32[6,2,512]{2,1,0:T(2,128)S(1)}) custom-call(bf16[512,768]{1,0:T(8,128)(2,1)S(1)} %copy-done.10, bf16[512,1536]{1,0:T(8,128)(2,1)S(1)} %fusion.23.k_ref.v_ref, bf16[512,1536]{1,0:T(8,128)(2,1)S(1)} %fusion.23.k_ref.v_ref, s32[1,512]{1,0:T(1,128)S(1)} %copy-done.50, ...), custom_call_target="tpu_custom_call" | custom-call | flops 512 | bytes 512 | tf_op jit(solution)/shard_map/attend_forward/pallas_call | solution.py:145
  73.6 8.1 %collective-permute-done.20 = bf16[520,768]{1,0:T(8,128)(2,1)} collective-permute-done((bf16[520,768]{1,0:T(8,128)(2,1)}, bf16[520,768]{1,0:T(8,128)(2,1)}, u32[]{:S(2)}, u32[]{:S(2)}) %collective-permute-start.20) | collective-permute-done | bytes 798752 | tf_op jit(solution)/shard_map/ppermute | solution.py:431
  86.6 8.9 %attend_forward.7 = (f32[768,512]{1,0:T(8,128)}, f32[6,2,512]{2,1,0:T(2,128)S(1)}, bf16[512,768]{1,0:T(8,128)(2,1)S(1)}) custom-call(bf16[512,768]{1,0:T(8,128)(2,1)S(1)} %copy-done.11, bf16[512,1536]{1,0:T(8,128)(2,1)} %fusion.24.k_ref.v_ref, bf16[512,1536]{1,0:T(8,128)(2,1)} %fusion.24.k_ref.v_ref, s32[1,512]{1,0:T(1,128)S(1)} %copy-done.50, ...), custom_call_target="tpu_custom_call" | custom-call | flops 512 | bytes 512 | tf_op jit(solution)/shard_map/attend_forward/pallas_call | solution.py:145
  98.8 5.6 %fusion.21 = (bf16[512,3072]{1,0:T(8,128)(2,1)S(1)}, bf16[512,3072]{1,0:T(8,128)(2,1)S(1)}) fusion(f32[3072]{0:T(1024)S(1)} %copy-done.65, bf16[768,3072]{1,0:T(8,128)(2,1)S(1)} %bitcast.80, f32[512,768]{1,0:T(8,128)S(1)} %subtract_multiply_fusion.3, f32[768]{0:T(1024)S(1)} %copy-done.69, f32[768]{0:T(1024)S(1)} %copy-done.54), kind=kOutput, calls=%fused_computation.70 | convolution fusion | flops 2435973120 | bytes 12601344 | tf_op jit(solution)/shard_map/dot_general | solution.py:25
  110.9 4.8 %convolution_convert_fusion.8 = bf16[3072,768]{1,0:T(8,128)(2,1)} fusion(bf16[512,3072]{1,0:T(8,128)(2,1)S(1)} %get-tuple-element.336, f32[512,768]{1,0:T(8,128)S(1)} %get-tuple-element.490), kind=kOutput, calls=%fused_computation.75 | convolution fusion | flops 2418671616 | bytes 9437184 | tf_op jit(solution)/shard_map/dot_general | solution.py:25
  120.2 4.3 %convolution_convert_fusion.7 = bf16[768,3072]{1,0:T(8,128)(2,1)} fusion(bf16[512,3072]{1,0:T(8,128)(2,1)S(1)} %multiply_convert_fusion, f32[512,768]{1,0:T(8,128)S(1)} %subtract_multiply_fusion.3, f32[768]{0:T(1024)S(1)} %copy-done.69, f32[768]{0:T(1024)S(1)} %copy-done.54), kind=kOutput, calls=%fused_computation.74 | convolution fusion | flops 2419458048 | bytes 9443328 | tf_op jit(solution)/shard_map/dot_general | solution.py:25
  125.7 87.7 %conditional.5 = (bf16[192,3072]{0,1:T(8,128)(2,1)}, bf16[192,3072]{0,1:T(8,128)(2,1)}, f32[768]{0:T(1024)S(1)}, f32[768]{0:T(1024)S(1)}, f32[768]{0:T(1024)S(1)...) conditional(s32[]{:T(128)} %bitcast.10, () %tuple.67, ...), branch_computations={%region_6.7_spmd, %region_7.0_spmd} | conditional | flops 14530513920 | bytes 284915552 | solution.py:355
  127.1 8.0 %multiply_reduce_fusion.1 = (f32[768]{0:T(1024)S(1)}, f32[512]{0:T(512)S(1)}, f32[512]{0:T(512)S(1)}, f32[768]{0:T(1024)S(1)}, f32[512,768]{1,0:T(8,128)S(1)}) fusion(f32[512,768]{1,0:T(8,128)S(1)} %get-tuple-element.146, f32[768]{0:T(1024)S(1)} %get-tuple-element.145, f32[512,768]{1,0:T(8,128)} %get-tuple-element.142, ...), kind=kOutput, calls=%fused_computation.26 | convolution fusion | flops 2419062272 | bytes 12596224 | tf_op jit(solution)/shard_map/cond/branch_1_fun/dot_general | solution.py:25
  138.5 11.6 %attend_backward.4 = (bf16[512,1536]{1,0:T(8,128)(2,1)S(1)}, f32[2,768]{1,0:T(2,128)S(1)}, f32[768,512]{1,0:T(8,128)S(1)}) custom-call(bf16[512,768]{1,0:T(8,128)(2,1)} %copy-done.12, bf16[512,768]{1,0:T(8,128)(2,1)S(1)} %convolution_convert_fusion.2.g_ref, bf16[512,1536]{1,0:T(8,128)(2,1)} %get-tuple-element.157.k_ref.v_ref, ...), custom_call_target="tpu_custom_call" | custom-call | flops 512 | bytes 512 | tf_op jit(solution)/shard_map/cond/branch_1_fun/attend_backward/pallas_call | solution.py:248
  150.1 10.6 %attend_backward.5 = (bf16[512,1536]{1,0:T(8,128)(2,1)S(1)}, f32[2,768]{1,0:T(2,128)S(1)}, f32[768,512]{1,0:T(8,128)S(1)}) custom-call(bf16[512,768]{1,0:T(8,128)(2,1)S(1)} %copy-done.13, bf16[512,768]{1,0:T(8,128)(2,1)S(1)} %convolution_convert_fusion.2.g_ref, bf16[512,1536]{1,0:T(8,128)(2,1)S(1)} %copy-done.18, bf16[512,1536]{1,0:T(8,128)(2,1)S(1)} %copy-done.18, ...), custom_call_target="tpu_custom_call" | custom-call | flops 512 | bytes 512 | tf_op jit(solution)/shard_map/cond/branch_1_fun/attend_backward/pallas_call | solution.py:248
  160.8 10.6 %attend_backward.6 = (bf16[512,1536]{1,0:T(8,128)(2,1)S(1)}, f32[2,768]{1,0:T(2,128)S(1)}, f32[768,512]{1,0:T(8,128)S(1)}) custom-call(bf16[512,768]{1,0:T(8,128)(2,1)S(1)} %copy-done.13, bf16[512,768]{1,0:T(8,128)(2,1)S(1)} %convolution_convert_fusion.2.g_ref, bf16[512,1536]{1,0:T(8,128)(2,1)S(1)} %copy-done.16, bf16[512,1536]{1,0:T(8,128)(2,1)S(1)} %copy-done.16, ...), custom_call_target="tpu_custom_call" | custom-call | flops 512 | bytes 512 | tf_op jit(solution)/shard_map/cond/branch_1_fun/attend_backward/pallas_call | solution.py:248
  171.4 11.7 %attend_backward.7 = (bf16[512,1536]{1,0:T(8,128)(2,1)S(1)}, f32[2,768]{1,0:T(2,128)S(1)}, bf16[512,768]{1,0:T(8,128)(2,1)S(1)}) custom-call(bf16[512,768]{1,0:T(8,128)(2,1)S(1)} %copy-done.13, bf16[512,768]{1,0:T(8,128)(2,1)S(1)} %convolution_convert_fusion.2.g_ref, bf16[512,1536]{1,0:T(8,128)(2,1)S(1)} %copy-done.14, bf16[512,1536]{1,0:T(8,128)(2,1)S(1)} %copy-done.14, ...), custom_call_target="tpu_custom_call" | custom-call | flops 512 | bytes 512 | tf_op jit(solution)/shard_map/cond/branch_1_fun/attend_backward/pallas_call | solution.py:248
  218.5 41.7 %conditional.6 = (bf16[96,3072]{1,0:T(8,128)(2,1)}, f32[12,768]{1,0:T(8,128)S(1)}, bf16[512,768]{1,0:T(8,128)(2,1)}, bf16[512,768]{1,0:T(8,128)(2,1)}, f32[512,768]{1,0:T(8,128)}, /*index=5*/f32[512,768]{1,0:T(8,128)}) conditional(s32[]{:T(128)} %bitcast.10, () %tuple.72, (bf16[192,3072]{0,1:T(8,128)(2,1)}, bf16[192,3072]{0,1:T(8,128)(2,1)}, ...), branch_computations={%region_13.14_spmd, %region_14.0_spmd} | conditional | flops 11425604 | bytes 57788404 | solution.py:355
  227.6 11.5 %collective-permute-done.9 = bf16[192,3072]{1,0:T(8,128)(2,1)} collective-permute-done((bf16[192,3072]{1,0:T(8,128)(2,1)}, bf16[192,3072]{1,0:T(8,128)(2,1)}, u32[]{:S(2)}, u32[]{:S(2)}) %collective-permute-start.9) | collective-permute-done | bytes 1179680 | tf_op jit(solution)/shard_map/cond/branch_1_fun/ppermute | solution.py:313
  245.6 4.2 %collective-permute-done.12 = f32[12,768]{1,0:T(8,128)S(1)} collective-permute-done((f32[12,768]{1,0:T(8,128)S(1)}, f32[12,768]{1,0:T(8,128)S(1)}, u32[]{:S(2)}, u32[]{:S(2)}) %collective-permute-start.12) | collective-permute-done | bytes 36896 | tf_op jit(solution)/shard_map/cond/branch_1_fun/ppermute | solution.py:313
  251.5 3.9 %fusion.1 = (f32[512,768]{1,0:T(8,128)}, f32[512,768]{1,0:T(8,128)}, bf16[512,768]{1,0:T(8,128)(2,1)}, bf16[512,768]{1,0:T(8,128)(2,1)}) fusion(bf16[512,768]{1,0:T(8,128)(2,1)} %get-tuple-element.192, bf16[512,768]{1,0:T(8,128)(2,1)} %get-tuple-element.191, pred[]{:T(512)S(6)} %eq.69, pred[]{:T(512)S(6)} %eq.68, pred[]{:T(512)S(6)} %eq.67, ...), kind=kLoop, calls=%fused_computation.7 | loop fusion | flops 3145728 | bytes 7077891 | tf_op jit(solution)/shard_map/convert_element_type | solution.py:33
  260.2 51.6 %conditional.7 = (bf16[96,3072]{1,0:T(8,128)(2,1)S(1)}, f32[12,768]{1,0:T(8,128)}, bf16[512,768]{1,0:T(8,128)(2,1)}, bf16[512,768]{1,0:T(8,128)(2,1)}, bf16[1,76...) conditional(s32[]{:T(128)} %bitcast.10, () %tuple.70, ...), branch_computations={%region_19.20_spmd, %region_20.21_spmd} | conditional | flops 8036404 | bytes 12866512 | solution.py:355
  261.3 9.1 %collective-permute-done.2 = bf16[48,3072]{1,0:T(8,128)(2,1)S(1)} collective-permute-done((bf16[48,3072]{1,0:T(8,128)(2,1)S(1)}, bf16[48,3072]{1,0:T(8,128)(2,1)S(1)}, u32[]{:S(2)}, u32[]{:S(2)}) %collective-permute-start.2) | collective-permute-done | bytes 294944 | tf_op jit(solution)/shard_map/cond/branch_1_fun/ppermute | solution.py:313
  271.6 12.8 %collective-permute-done.3 = bf16[24,3072]{1,0:T(8,128)(2,1)S(1)} collective-permute-done((bf16[24,3072]{1,0:T(8,128)(2,1)S(1)}, bf16[24,3072]{1,0:T(8,128)(2,1)S(1)}, u32[]{:S(2)}, u32[]{:S(2)}) %collective-permute-start.3) | collective-permute-done | bytes 147488 | tf_op jit(solution)/shard_map/cond/branch_1_fun/ppermute | solution.py:313
  285.2 8.3 %collective-permute-done.6 = f32[12,768]{1,0:T(8,128)S(1)} collective-permute-done((f32[12,768]{1,0:T(8,128)S(1)}, f32[12,768]{1,0:T(8,128)S(1)}, u32[]{:S(2)}, u32[]{:S(2)}) %collective-permute-start.6) | collective-permute-done | bytes 36896 | tf_op jit(solution)/shard_map/cond/branch_1_fun/ppermute | solution.py:313
  304.1 7.7 %collective-permute-done.5 = bf16[48,3072]{1,0:T(8,128)(2,1)S(1)} collective-permute-done((bf16[48,3072]{1,0:T(8,128)(2,1)S(1)}, bf16[48,3072]{1,0:T(8,128)(2,1)S(1)}, u32[]{:S(2)}, u32[]{:S(2)}) %collective-permute-start.5) | collective-permute-done | bytes 294944 | tf_op jit(solution)/shard_map/cond/branch_1_fun/ppermute | solution.py:313
  316.9 30.0 %conditional.8 = (bf16[384,3072]{1,0:T(8,128)(2,1)S(1)}) conditional(s32[]{:T(128)} %bitcast.10, () %tuple.77, bf16[96,3072]{1,0:T(8,128)(2,1)S(1)} %get-tuple-element.369), branch_computations={%region_21.22_spmd, %region_22.23_spmd} | conditional | flops 15925307 | bytes 16515783 | solution.py:355
  318.5 8.4 %collective-permute-done = bf16[96,3072]{1,0:T(8,128)(2,1)S(1)} collective-permute-done((bf16[96,3072]{1,0:T(8,128)(2,1)S(1)}, bf16[96,3072]{1,0:T(8,128)(2,1)S(1)}, u32[]{:S(2)}, u32[]{:S(2)}) %collective-permute-start) | collective-permute-done | bytes 589856 | tf_op jit(solution)/shard_map/cond/branch_1_fun/ppermute | solution.py:313
  329.9 15.0 %collective-permute-done.1 = bf16[192,3072]{1,0:T(8,128)(2,1)} collective-permute-done((bf16[192,3072]{1,0:T(8,128)(2,1)S(1)}, bf16[192,3072]{1,0:T(8,128)(2,1)}, u32[]{:S(2)}, u32[]{:S(2)}) %collective-permute-start.1) | collective-permute-done | bytes 1179680 | tf_op jit(solution)/shard_map/cond/branch_1_fun/ppermute | solution.py:313
  352.6 6.9 %collective-permute-start.26 = (bf16[512,768]{1,0:T(8,128)(2,1)S(1)}, bf16[512,768]{1,0:T(8,128)(2,1)}, u32[]{:S(2)}, u32[]{:S(2)}) collective-permute-start(bf16[512,768]{1,0:T(8,128)(2,1)S(1)} %add_convert_fusion.9), channel_id=1, source_target_pairs={{0,1},{1,2},{2,3},{4,5},{5,6},{6,7},{8,9},{9,10},{10,11},{12,13},{... | collective-permute-start | bytes 2359304 | tf_op jit(solution)/shard_map/ppermute | solution.py:512
  359.5 19.5 %conditional.9 = (f32[768,768]{1,0:T(8,128)}, f32[768,768]{1,0:T(8,128)}, f32[768,768]{1,0:T(8,128)}, f32[768,768]{1,0:T(8,128)}, f32[3072,768]{1,0:T(8,128)}, /*index=5*/f32[768,3072]{1,0:T(8,128)}) conditional(s32[]{:T(128)} %bitcast.10, () %tuple.80, (bf16[384,3072]{1,0:T(8,128)(2,1)S(1)}, bf16[3072,768]{1,0:T(8,128)(2,1)}, ...), branch_computations={%region_25.26_spmd, %region_26.27_spmd} | conditional | flops 28311568 | bytes 80216320 | solution.py:355
  359.7 7.0 %convert_element_type.201 = f32[3072,768]{1,0:T(8,128)} convert(bf16[3072,768]{1,0:T(8,128)(2,1)} %get-tuple-element.200) | non-fusion elementwise | flops 2359296 | bytes 14155776 | tf_op jit(solution)/shard_map/cond/branch_1_fun/convert_element_type | solution.py:33
  366.7 5.0 %convert_element_type.202 = f32[768,3072]{1,0:T(8,128)} convert(bf16[768,3072]{1,0:T(8,128)(2,1)S(1)} %copy-done.28) | non-fusion elementwise | flops 2359296 | bytes 14155776 | tf_op jit(solution)/shard_map/cond/branch_1_fun/convert_element_type | solution.py:33
  (310 shorter events, 150.1 us)
Async XLA Ops:
  7.2 352.3 %all-reduce.5.cloned.1.call-start = ((), (), s32[]{:S(2)}) async-start(), calls=%async_computation | async-start | bytes 18874368 | tf_op jit(solution)/shard_map/psum | solution.py:464
  9.3 23.0 %collective-permute-start.16 = (bf16[520,768]{1,0:T(8,128)(2,1)S(1)}, bf16[520,768]{1,0:T(8,128)(2,1)}, u32[]{:S(2)}, u32[]{:S(2)}) collective-permute-start(bf16[520,768]{1,0:T(8,128)(2,1)S(1)} %pad_maximum_fusion.1), channel_id=1, source_target_pairs={{1,0},{2,1},{3,2},{5,4},{6,5},{7,6},{9,8},{10,9},{11,10},{13,12},{... | collective-permute-start | bytes 2396168 | tf_op jit(solution)/shard_map/ppermute | solution.py:431
  10.7 22.6 %collective-permute-start.15 = (bf16[520,768]{1,0:T(8,128)(2,1)S(1)}, bf16[520,768]{1,0:T(8,128)(2,1)}, u32[]{:S(2)}, u32[]{:S(2)}) collective-permute-start(bf16[520,768]{1,0:T(8,128)(2,1)S(1)} %pad_maximum_fusion.1), channel_id=1, source_target_pairs={{0,1},{1,2},{2,3},{4,5},{5,6},{6,7},{8,9},{9,10},{10,11},{12,13},{... | collective-permute-start | bytes 2396168 | tf_op jit(solution)/shard_map/ppermute | solution.py:430
  33.3 15.0 %collective-permute-start.17 = (bf16[520,768]{1,0:T(8,128)(2,1)}, bf16[520,768]{1,0:T(8,128)(2,1)}, u32[]{:S(2)}, u32[]{:S(2)}) collective-permute-start(bf16[520,768]{1,0:T(8,128)(2,1)} %collective-permute-done.15), channel_id=1, source_target_pairs={{1,2},{2,3},{5,6},{6,7},{9,10},{10,11},{13,14},{14,15},{17,18},{18... | collective-permute-start | bytes 2396168 | tf_op jit(solution)/shard_map/ppermute | solution.py:430
  34.9 24.1 %collective-permute-start.18 = (bf16[520,768]{1,0:T(8,128)(2,1)}, bf16[520,768]{1,0:T(8,128)(2,1)}, u32[]{:S(2)}, u32[]{:S(2)}) collective-permute-start(bf16[520,768]{1,0:T(8,128)(2,1)} %collective-permute-done.16), channel_id=1, source_target_pairs={{1,0},{2,1},{5,4},{6,5},{9,8},{10,9},{13,12},{14,13},{17,16},{18,1... | collective-permute-start | bytes 2396168 | tf_op jit(solution)/shard_map/ppermute | solution.py:431
  59.0 14.6 %collective-permute-start.19 = (bf16[520,768]{1,0:T(8,128)(2,1)}, bf16[520,768]{1,0:T(8,128)(2,1)}, u32[]{:S(2)}, u32[]{:S(2)}) collective-permute-start(bf16[520,768]{1,0:T(8,128)(2,1)} %collective-permute-done.17), channel_id=1, source_target_pairs={{2,3},{6,7},{10,11},{14,15},{18,19},{22,23},{26,27},{30,31}} | collective-permute-start | bytes 2396168 | tf_op jit(solution)/shard_map/ppermute | solution.py:430
  62.1 19.6 %collective-permute-start.20 = (bf16[520,768]{1,0:T(8,128)(2,1)}, bf16[520,768]{1,0:T(8,128)(2,1)}, u32[]{:S(2)}, u32[]{:S(2)}) collective-permute-start(bf16[520,768]{1,0:T(8,128)(2,1)} %collective-permute-done.18), channel_id=1, source_target_pairs={{1,0},{5,4},{9,8},{13,12},{17,16},{21,20},{25,24},{29,28}} | collective-permute-start | bytes 2396168 | tf_op jit(solution)/shard_map/ppermute | solution.py:431
  160.7 25.6 %copy-start = (bf16[512,1536]{1,0:T(8,128)(2,1)}, bf16[512,1536]{1,0:T(8,128)(2,1)S(1)}, u32[]{:S(2)}) copy-start(bf16[512,1536]{1,0:T(8,128)(2,1)S(1)} %get-tuple-element.166) | copy-start | bytes 4718596 | tf_op jit(solution)/shard_map/cond
  171.4 16.4 %copy-start.2 = (bf16[512,1536]{1,0:T(8,128)(2,1)}, bf16[512,1536]{1,0:T(8,128)(2,1)S(1)}, u32[]{:S(2)}) copy-start(bf16[512,1536]{1,0:T(8,128)(2,1)S(1)} %get-tuple-element.168) | copy-start | bytes 4718596 | tf_op jit(solution)/shard_map/cond
  194.4 13.0 %collective-permute-start.14 = (bf16[384,3072]{0,1:T(8,128)(2,1)}, bf16[384,3072]{0,1:T(8,128)(2,1)}, u32[]{:S(2)}, u32[]{:S(2)}) collective-permute-start(bf16[384,3072]{0,1:T(8,128)(2,1)} %constant_dynamic-slice_fusion.3), channel_id=1, source_target_pairs={{0,4},{4,0},{8,12},{12,8},{16,20},{20,16},{24,28},{28,24},{1,5},{5... | collective-permute-start | bytes 7077896 | tf_op jit(solution)/shard_map/cond/branch_1_fun/ppermute | solution.py:313
  213.4 46.9 %collective-permute-start.21 = (bf16[512,768]{1,0:T(8,128)(2,1)}, bf16[512,768]{1,0:T(8,128)(2,1)}, u32[]{:S(2)}, u32[]{:S(2)}) collective-permute-start(bf16[512,768]{1,0:T(8,128)(2,1)} %get-tuple-element.346), channel_id=1, source_target_pairs={{3,2},{7,6},{11,10},{15,14},{19,18},{23,22},{27,26},{31,30}} | collective-permute-start | bytes 2359304 | tf_op jit(solution)/shard_map/ppermute | solution.py:511
  215.1 45.2 %collective-permute-start.22 = (bf16[512,768]{1,0:T(8,128)(2,1)}, bf16[512,768]{1,0:T(8,128)(2,1)}, u32[]{:S(2)}, u32[]{:S(2)}) collective-permute-start(bf16[512,768]{1,0:T(8,128)(2,1)} %get-tuple-element.346), channel_id=1, source_target_pairs={{0,1},{4,5},{8,9},{12,13},{16,17},{20,21},{24,25},{28,29}} | collective-permute-start | bytes 2359304 | tf_op jit(solution)/shard_map/ppermute | solution.py:512
  221.0 18.1 %collective-permute-start.9 = (bf16[192,3072]{1,0:T(8,128)(2,1)}, bf16[192,3072]{1,0:T(8,128)(2,1)}, u32[]{:S(2)}, u32[]{:S(2)}) collective-permute-start(bf16[192,3072]{1,0:T(8,128)(2,1)} %copy.48), channel_id=1, source_target_pairs={{0,8},{4,20},{8,0},{12,28},{16,24},{20,4},{24,16},{28,12},{1,9},{5... | collective-permute-start | bytes 3538952 | tf_op jit(solution)/shard_map/cond/branch_1_fun/ppermute | solution.py:313
  226.9 12.2 %copy-start.29 = (bf16[192,3072]{1,0:T(8,128)(2,1)S(1)}, bf16[192,3072]{1,0:T(8,128)(2,1)}, u32[]{:S(2)}) copy-start(bf16[192,3072]{1,0:T(8,128)(2,1)} %copy.47) | copy-start | bytes 3538948 | tf_op jit(solution)/shard_map/cond
  227.6 14.9 %copy-start.26 = (f32[512,768]{1,0:T(8,128)S(1)}, f32[512,768]{1,0:T(8,128)}, u32[]{:S(2)}) copy-start(f32[512,768]{1,0:T(8,128)} %get-tuple-element.185) | copy-start | bytes 4718596 | tf_op jit(solution)/shard_map/cond
  240.8 17.3 %collective-permute-start.10 = (bf16[96,3072]{1,0:T(8,128)(2,1)S(1)}, bf16[96,3072]{1,0:T(8,128)(2,1)}, u32[]{:S(2)}, u32[]{:S(2)}) collective-permute-start(bf16[96,3072]{1,0:T(8,128)(2,1)S(1)} %constant_dynamic-slice_fusion), channel_id=1, source_target_pairs={{0,16},{4,12},{8,24},{12,4},{16,0},{20,28},{24,8},{28,20},{1,17},{... | collective-permute-start | bytes 1769480 | tf_op jit(solution)/shard_map/cond/branch_1_fun/ppermute | solution.py:313
  242.7 1.6 collective-permute-start.11
  244.4 5.5 %collective-permute-start.12 = (f32[12,768]{1,0:T(8,128)S(1)}, f32[12,768]{1,0:T(8,128)S(1)}, u32[]{:S(2)}, u32[]{:S(2)}) collective-permute-start(f32[12,768]{1,0:T(8,128)S(1)} %add.278), channel_id=1, source_target_pairs={{0,8},{4,20},{8,0},{12,28},{16,24},{20,4},{24,16},{28,12},{1,9},{5... | collective-permute-start | bytes 110600 | tf_op jit(solution)/shard_map/cond/branch_1_fun/ppermute | solution.py:313
  249.9 8.3 %collective-permute-start.13 = (f32[12,768]{1,0:T(8,128)S(1)}, f32[12,768]{1,0:T(8,128)S(1)}, u32[]{:S(2)}, u32[]{:S(2)}) collective-permute-start(f32[12,768]{1,0:T(8,128)S(1)} %add.279), channel_id=1, source_target_pairs={{0,16},{4,12},{8,24},{12,4},{16,0},{20,28},{24,8},{28,20},{1,17},{... | collective-permute-start | bytes 110600 | tf_op jit(solution)/shard_map/cond/branch_1_fun/ppermute | solution.py:313
  261.2 9.2 %collective-permute-start.2 = (bf16[48,3072]{1,0:T(8,128)(2,1)S(1)}, bf16[48,3072]{1,0:T(8,128)(2,1)S(1)}, u32[]{:S(2)}, u32[]{:S(2)}) collective-permute-start(bf16[48,3072]{1,0:T(8,128)(2,1)S(1)} %constant_dynamic-slice_fusion.5), channel_id=1, source_target_pairs={{0,1},{1,0},{2,3},{3,2},{4,5},{5,4},{6,7},{7,6},{8,9},{9,8},{10,11... | collective-permute-start | bytes 884744 | tf_op jit(solution)/shard_map/cond/branch_1_fun/ppermute | solution.py:313
  271.5 12.9 %collective-permute-start.3 = (bf16[24,3072]{1,0:T(8,128)(2,1)S(1)}, bf16[24,3072]{1,0:T(8,128)(2,1)S(1)}, u32[]{:S(2)}, u32[]{:S(2)}) collective-permute-start(bf16[24,3072]{1,0:T(8,128)(2,1)S(1)} %constant_dynamic-slice_fusion.4), channel_id=1, source_target_pairs={{0,2},{1,3},{2,0},{3,1},{4,6},{5,7},{6,4},{7,5},{8,10},{9,11},{10,... | collective-permute-start | bytes 442376 | tf_op jit(solution)/shard_map/cond/branch_1_fun/ppermute | solution.py:313
  284.5 12.0 %collective-permute-start.4 = (bf16[24,3072]{1,0:T(8,128)(2,1)S(1)}, bf16[24,3072]{1,0:T(8,128)(2,1)S(1)}, u32[]{:S(2)}, u32[]{:S(2)}) collective-permute-start(bf16[24,3072]{1,0:T(8,128)(2,1)S(1)} %add_convert_fusion.7), channel_id=1, source_target_pairs={{0,2},{1,3},{2,0},{3,1},{4,6},{5,7},{6,4},{7,5},{8,10},{9,11},{10,... | collective-permute-start | bytes 442376 | tf_op jit(solution)/shard_map/cond/branch_1_fun/ppermute | solution.py:313
  284.6 8.9 %collective-permute-start.6 = (f32[12,768]{1,0:T(8,128)S(1)}, f32[12,768]{1,0:T(8,128)S(1)}, u32[]{:S(2)}, u32[]{:S(2)}) collective-permute-start(f32[12,768]{1,0:T(8,128)S(1)} %get-tuple-element.194), channel_id=1, source_target_pairs={{0,1},{1,0},{2,3},{3,2},{4,5},{5,4},{6,7},{7,6},{8,9},{9,8},{10,11... | collective-permute-start | bytes 110600 | tf_op jit(solution)/shard_map/cond/branch_1_fun/ppermute | solution.py:313
  293.5 6.7 %collective-permute-start.7 = (f32[12,768]{1,0:T(8,128)S(1)}, f32[12,768]{1,0:T(8,128)S(1)}, u32[]{:S(2)}, u32[]{:S(2)}) collective-permute-start(f32[12,768]{1,0:T(8,128)S(1)} %add.289), channel_id=1, source_target_pairs={{0,2},{1,3},{2,0},{3,1},{4,6},{5,7},{6,4},{7,5},{8,10},{9,11},{10,... | collective-permute-start | bytes 110600 | tf_op jit(solution)/shard_map/cond/branch_1_fun/ppermute | solution.py:313
  296.6 15.2 %collective-permute-start.5 = (bf16[48,3072]{1,0:T(8,128)(2,1)S(1)}, bf16[48,3072]{1,0:T(8,128)(2,1)S(1)}, u32[]{:S(2)}, u32[]{:S(2)}) collective-permute-start(bf16[48,3072]{1,0:T(8,128)(2,1)S(1)} %maximum_select_fusion.7), channel_id=1, source_target_pairs={{0,1},{1,0},{2,3},{3,2},{4,5},{5,4},{6,7},{7,6},{8,9},{9,8},{10,11... | collective-permute-start | bytes 884744 | tf_op jit(solution)/shard_map/cond/branch_1_fun/ppermute | solution.py:313
  312.0 34.9 %collective-permute-start.23 = (bf16[512,768]{1,0:T(8,128)(2,1)}, bf16[512,768]{1,0:T(8,128)(2,1)}, u32[]{:S(2)}, u32[]{:S(2)}) collective-permute-start(bf16[512,768]{1,0:T(8,128)(2,1)} %get-tuple-element.367), channel_id=1, source_target_pairs={{2,1},{3,2},{6,5},{7,6},{10,9},{11,10},{14,13},{15,14},{18,17},{19... | collective-permute-start | bytes 2359304 | tf_op jit(solution)/shard_map/ppermute | solution.py:511
  313.6 33.3 %collective-permute-start.24 = (bf16[512,768]{1,0:T(8,128)(2,1)}, bf16[512,768]{1,0:T(8,128)(2,1)}, u32[]{:S(2)}, u32[]{:S(2)}) collective-permute-start(bf16[512,768]{1,0:T(8,128)(2,1)} %get-tuple-element.368), channel_id=1, source_target_pairs={{0,1},{1,2},{4,5},{5,6},{8,9},{9,10},{12,13},{13,14},{16,17},{17,1... | collective-permute-start | bytes 2359304 | tf_op jit(solution)/shard_map/ppermute | solution.py:512
  316.9 9.9 %collective-permute-start = (bf16[96,3072]{1,0:T(8,128)(2,1)S(1)}, bf16[96,3072]{1,0:T(8,128)(2,1)S(1)}, u32[]{:S(2)}, u32[]{:S(2)}) collective-permute-start(bf16[96,3072]{1,0:T(8,128)(2,1)S(1)} %param.7), channel_id=1, source_target_pairs={{0,16},{4,12},{8,24},{12,4},{16,0},{20,28},{24,8},{28,20},{1,17},{... | collective-permute-start | bytes 1769480 | tf_op jit(solution)/shard_map/cond/branch_1_fun/ppermute | solution.py:313
  328.4 16.4 %collective-permute-start.1 = (bf16[192,3072]{1,0:T(8,128)(2,1)S(1)}, bf16[192,3072]{1,0:T(8,128)(2,1)}, u32[]{:S(2)}, u32[]{:S(2)}) collective-permute-start(bf16[192,3072]{1,0:T(8,128)(2,1)S(1)} %maximum_select_fusion.1), channel_id=1, source_target_pairs={{0,8},{4,20},{8,0},{12,28},{16,24},{20,4},{24,16},{28,12},{1,9},{5... | collective-permute-start | bytes 3538952 | tf_op jit(solution)/shard_map/cond/branch_1_fun/ppermute | solution.py:313
  351.3 27.7 %collective-permute-start.25 = (bf16[512,768]{1,0:T(8,128)(2,1)}, bf16[512,768]{1,0:T(8,128)(2,1)}, u32[]{:S(2)}, u32[]{:S(2)}) collective-permute-start(bf16[512,768]{1,0:T(8,128)(2,1)} %add_convert_fusion.10), channel_id=1, source_target_pairs={{1,0},{2,1},{3,2},{5,4},{6,5},{7,6},{9,8},{10,9},{11,10},{13,12},{... | collective-permute-start | bytes 2359304 | tf_op jit(solution)/shard_map/ppermute | solution.py:511
  352.6 26.4 %collective-permute-start.26 = (bf16[512,768]{1,0:T(8,128)(2,1)S(1)}, bf16[512,768]{1,0:T(8,128)(2,1)}, u32[]{:S(2)}, u32[]{:S(2)}) collective-permute-start(bf16[512,768]{1,0:T(8,128)(2,1)S(1)} %add_convert_fusion.9), channel_id=1, source_target_pairs={{0,1},{1,2},{2,3},{4,5},{5,6},{6,7},{8,9},{9,10},{10,11},{12,13},{... | collective-permute-start | bytes 2359304 | tf_op jit(solution)/shard_map/ppermute | solution.py:512
  359.6 12.3 %collective-permute-start.8 = (bf16[384,3072]{1,0:T(8,128)(2,1)S(1)}, bf16[384,3072]{1,0:T(8,128)(2,1)}, u32[]{:S(2)}, u32[]{:S(2)}) collective-permute-start(bf16[384,3072]{1,0:T(8,128)(2,1)S(1)} %get-tuple-element.199), channel_id=1, source_target_pairs={{0,4},{4,0},{8,12},{12,8},{16,20},{20,16},{24,28},{28,24},{1,5},{5... | collective-permute-start | bytes 7077896 | tf_op jit(solution)/shard_map/cond/branch_1_fun/ppermute | solution.py:313
  (72 other events, 313.8 us)
Sparse Core Ops, SparseCore 0:
  124.6 219.7 all-reduce.4
